TPU v7x, 32 devices: a whole 2x2x4 slice. The times are simulated.
32 devices in a mesh: row: 2 (over x), col: 16 (over z, y, core).
Axes of the slice: x: 2, y: 2, z: 4, core: 2. Of those that a mesh axis runs over, the one named last changes fastest.
Arguments:
- contexts: bfloat16 [4096, 128], P(('row', 'col')), may hold values from -8 to 8
- logged_actions: int32 [4096], P(('row', 'col')), may hold values from 0 to 131041
- policy_actions: int32 [4096, 8], P(('row', 'col')), may hold values from 0 to 131041
- rewards: float32 [4096], P(('row', 'col')), may hold values from 0.2 to 2
Outputs:
- weights: float32 [4096, 8], P(('row', 'col'))
- residual: float32 [4096, 8], P(('row', 'col'))
- values: float32 [8], replicated
All inputs are finite; a program needn't handle non-finite values.
Results may differ from a plain program's by a relative error of at most 0.0056.
Values may be sent and summed in bfloat16 or wider, within the bound.
A program may use at most 64 MiB of HBM per device.

v0:
```python
import math

import jax
import jax.numpy as jnp
from jax import lax
from jax.sharding import PartitionSpec as P

NPOL = 8
NACT = 16
CATALOG = 131042


ridge = 0.1
group_size = 16
stride_base = 1009
phase_step = 0.37
two_pi = 2.0 * math.pi


def action_features(chosen, width):
    levels = jnp.arange(width, dtype=jnp.int32)
    multipliers = 1 + stride_base * levels
    turned = chosen[..., None] * multipliers % CATALOG
    angles = turned.astype(jnp.float32) * (two_pi / CATALOG) + phase_step * levels.astype(
        jnp.float32
    )
    wave_terms = math.sqrt(2.0 / width) * jnp.cos(angles)
    constant_term = jnp.full(wave_terms.shape, 1.0 / math.sqrt(width), jnp.float32)
    return jnp.where(levels == 0, constant_term, wave_terms).astype(jnp.bfloat16)


def select_actions(products, onehot):
    shaped = products.reshape(
        products.shape[:-1] + (products.shape[-1] // onehot.shape[-1], onehot.shape[-1])
    )
    return jnp.sum(shaped * jnp.expand_dims(onehot.astype(jnp.float32), -2), axis=-1)


def kernel_tiles(left_tiles, right_tiles, left_squares, right_squares):
    inner = jnp.einsum("grd,gsd->grs", left_tiles, right_tiles, preferred_element_type=jnp.float32)
    expo = (2.0 * inner - left_squares[:, :, None] - right_squares[:, None, :]) / left_tiles.shape[
        -1
    ]
    return jnp.exp(expo).astype(jnp.bfloat16)


def tile_terms(kernel, left_matrix, right_matrix, left_onehot, right_onehot):
    toward_left = jnp.einsum(
        "grs,gsm->grm", kernel, right_matrix, preferred_element_type=jnp.float32
    )
    toward_right = jnp.einsum(
        "grs,grm->gsm", kernel, left_matrix, preferred_element_type=jnp.float32
    )
    return (select_actions(toward_left, left_onehot), select_actions(toward_right, right_onehot))


def listed_pass(
    left_ctx,
    left_squares,
    left_matrix,
    left_onehot,
    right_ctx,
    right_squares,
    right_matrix,
    right_onehot,
    placed,
    diagonal,
):
    left_count = left_ctx.shape[0]
    tile_rows = left_ctx.shape[1]
    right_count = right_ctx.shape[0]
    policies = left_matrix.shape[-1] // left_onehot.shape[-1]
    flat_placed = placed.reshape(-1)
    flat_diagonal = diagonal.reshape(-1)
    plan = jnp.argsort(1 - flat_placed, stable=True)
    active_count = jnp.sum(flat_placed)
    rounds = (active_count + group_size - 1) // group_size

    def advance(round_index, carried):
        row_sums, column_sums = carried
        picked = lax.dynamic_slice_in_dim(plan, round_index * group_size, group_size)
        left_pick = picked // right_count
        right_pick = picked % right_count
        live_flags = jnp.take(flat_placed, picked).astype(jnp.float32)
        mirror_flags = live_flags * (1 - jnp.take(flat_diagonal, picked)).astype(jnp.float32)
        kernel = kernel_tiles(
            left_ctx[left_pick],
            right_ctx[right_pick],
            left_squares[left_pick],
            right_squares[right_pick],
        )
        toward_left, toward_right = tile_terms(
            kernel,
            left_matrix[left_pick],
            right_matrix[right_pick],
            left_onehot[left_pick],
            right_onehot[right_pick],
        )
        row_sums = row_sums.at[left_pick].add(toward_left * live_flags[:, None, None])
        column_sums = column_sums.at[right_pick].add(toward_right * mirror_flags[:, None, None])
        return (row_sums, column_sums)

    start_rows = jnp.zeros((left_count, tile_rows, policies), jnp.float32)
    start_columns = jnp.zeros((right_count, tile_rows, policies), jnp.float32)
    return lax.fori_loop(0, rounds, advance, (start_rows, start_columns))


def on_device(contexts, logged_actions, policy_actions, rewards):
    tile_rows, feature_count = contexts.shape
    left_count = lax.axis_size("col")
    right_count = lax.axis_size("row")
    factor = NACT / (tile_rows * left_count * right_count)
    own_column = lax.axis_index("col")
    own_row = lax.axis_index("row")
    left_ids = jnp.arange(left_count, dtype=jnp.int32)[:, None]
    right_ids = jnp.arange(right_count, dtype=jnp.int32)[None, :]
    first_owner = own_row * left_count + left_ids
    second_owner = right_ids * left_count + own_column
    parity = (first_owner + second_owner) % 2
    placed = jnp.where(
        first_owner == second_owner, 1, jnp.where(first_owner < second_owner, parity, 1 - parity)
    )
    diagonal = ((left_ids == own_column) & (right_ids == own_row)).astype(jnp.int32)
    left_logged, left_policy = (
        lax.all_gather(logged_actions, "col", axis=0, tiled=True),
        lax.all_gather(policy_actions, "col", axis=0, tiled=True),
    )
    right_logged, right_policy = (
        lax.all_gather(logged_actions, "row", axis=0, tiled=True),
        lax.all_gather(policy_actions, "row", axis=0, tiled=True),
    )
    left_onehot = action_features(left_logged, NACT).reshape(left_count, tile_rows, NACT)
    right_onehot = action_features(right_logged, NACT).reshape(right_count, tile_rows, NACT)
    left_first = action_features(left_policy, NACT).reshape(left_count, tile_rows, NPOL * NACT)
    right_first = action_features(right_policy, NACT).reshape(right_count, tile_rows, NPOL * NACT)
    right_ctx = lax.all_gather(contexts, "row", axis=0, tiled=True).reshape(
        right_count, tile_rows, feature_count
    )
    right_squares = jnp.sum(right_ctx.astype(jnp.float32) ** 2, axis=2)
    left_ctx = lax.all_gather(contexts, "col", axis=0, tiled=True).reshape(
        left_count, tile_rows, feature_count
    )
    left_squares = jnp.sum(left_ctx.astype(jnp.float32) ** 2, axis=2)

    def sweep(left_matrix, right_matrix):
        return listed_pass(
            left_ctx,
            left_squares,
            left_matrix,
            left_onehot,
            right_ctx,
            right_squares,
            right_matrix,
            right_onehot,
            placed,
            diagonal,
        )

    def reduce_terms(toward_left, toward_right):
        mine_left = lax.psum_scatter(toward_left, "col", scatter_dimension=0, tiled=True)
        mine_right = lax.psum_scatter(toward_right, "row", scatter_dimension=0, tiled=True)
        return factor * (mine_left[0] + mine_right[0])

    first_left, first_right = sweep(left_first, right_first)
    right_side = reduce_terms(first_left, first_right)
    right_low = right_side.astype(jnp.bfloat16)
    left_rhs = lax.all_gather(right_low, "col", axis=0, tiled=True).reshape(
        left_count, tile_rows, NPOL
    )
    right_rhs = lax.all_gather(right_low, "row", axis=0, tiled=True).reshape(
        right_count, tile_rows, NPOL
    )
    left_second = (left_onehot[:, :, None, :] * left_rhs[:, :, :, None]).reshape(
        left_count, tile_rows, NPOL * NACT
    )
    right_second = (right_onehot[:, :, None, :] * right_rhs[:, :, :, None]).reshape(
        right_count, tile_rows, NPOL * NACT
    )
    second_left, second_right = sweep(left_second, right_second)
    image = reduce_terms(second_left, second_right) + ridge * right_side
    norm_sums, curvature, reward_sums = lax.psum(
        (
            jnp.sum(right_side * right_side, axis=0),
            jnp.sum(right_side * image, axis=0),
            jnp.sum(rewards[:, None] * right_side, axis=0),
        ),
        ("row", "col"),
    )
    alpha = norm_sums / curvature
    weights = alpha[None, :] * right_side
    residual = right_side - alpha[None, :] * image
    values = alpha * reward_sums / (tile_rows * left_count * right_count)
    return (weights, residual, values)


def solution(mesh):
    placed = (
        P(("row", "col"), None),
        P(("row", "col")),
        P(("row", "col"), None),
        P(("row", "col")),
    )
    return jax.shard_map(
        on_device,
        mesh=mesh,
        in_specs=placed,
        out_specs=(P(("row", "col"), None), P(("row", "col"), None), P()),
        check_vma=False,
    )
```

profile of v0, /device:TPU:0, one launch (start us, length us, event | category | flops | bytes accessed | tf_op | source)
XLA Modules:
  0.0 402.4 jit_solution(18050455867329643526)
XLA Ops:
  7.2 0.7 broadcast_add_fusion.2
  8.7 0.6 copy-done.21
  9.4 23.0 %all-gather = s32[16,1,128]{2,1,0:T(1,128)S(1)} all-gather(s32[1,1,128]{2,1,0:T(1,128)S(1)} %bitcast.103), channel_id=1, replica_groups=mesh['row'=2,'col'=16] {'col'}, dimensions={0}, use_global_device_ids=true | all-gather | bytes 8704 | tf_op jit(solution)/shard_map/all_gather | solution.py:125
  32.4 4.2 %all-gather.1 = s32[2,1,128]{2,1,0:T(1,128)S(1)} all-gather(s32[1,1,128]{2,1,0:T(1,128)S(1)} %bitcast.104), channel_id=1, replica_groups=mesh['row'=2,'col'=16] {'row'}, dimensions={0}, use_global_device_ids=true | all-gather | bytes 1536 | tf_op jit(solution)/shard_map/all_gather | solution.py:129
  36.6 18.7 %all_gather.24 = bf16[2048,128]{1,0:T(8,128)(2,1)S(1)} all-gather(bf16[128,128]{1,0:T(8,128)(2,1)S(1)} %copy-done.4), channel_id=1, replica_groups=mesh['row'=2,'col'=16] {'col'}, dimensions={0}, use_global_device_ids=true | all-gather | bytes 557056 | tf_op jit(solution)/shard_map/all_gather | solution.py:140
  55.3 4.7 %all_gather.25 = bf16[256,128]{1,0:T(8,128)(2,1)S(1)} all-gather(bf16[128,128]{1,0:T(8,128)(2,1)S(1)} %copy-done.4), channel_id=1, replica_groups=mesh['row'=2,'col'=16] {'row'}, dimensions={0}, use_global_device_ids=true | all-gather | bytes 98304 | tf_op jit(solution)/shard_map/all_gather | solution.py:136
  60.0 19.1 %all_gather.28 = s32[2048,8]{0,1:T(8,128)S(1)} all-gather(s32[128,8]{0,1:T(8,128)S(1)} %copy-done.20), channel_id=1, replica_groups=mesh['row'=2,'col'=16] {'col'}, dimensions={0}, use_global_device_ids=true | all-gather | bytes 69632 | tf_op jit(solution)/shard_map/all_gather | solution.py:126
  79.1 4.3 %all_gather.26 = s32[256,8]{0,1:T(8,128)S(1)} all-gather(s32[128,8]{0,1:T(8,128)S(1)} %copy-done.20), channel_id=1, replica_groups=mesh['row'=2,'col'=16] {'row'}, dimensions={0}, use_global_device_ids=true | all-gather | bytes 12288 | tf_op jit(solution)/shard_map/all_gather | solution.py:130
  83.8 0.6 broadcast_in_dim.77
  84.4 0.6 add.297
  85.5 1.6 sort.19
  87.1 22.2 %while.32 = (s32[]{:T(128)}, f32[16,128,8]{1,2,0:T(8,128)S(1)}, f32[2,128,8]{1,2,0:T(8,128)S(1)}, s32[]{:T(128)}, s32[32]{0:T(128)S(1)}, /*index=5*/bf16[16,128,...) while((s32[]{:T(128)}, f32[16,128,8]{1,2,0:T(8,128)S(1)}, ...), condition=%wide.region_9.11_spmd.clone.clone, body=%wide.region_4.10_spmd.clone.clone.sunk | while | flops 208101696 | bytes 17992608 | solution.py:105
  87.3 0.6 copy-done.5
  87.9 0.6 gather_fusion.2
  88.5 0.6 gather_fusion.3
  89.7 0.6 gather_fusion.1
  90.3 0.6 gather_fusion.4
  91.6 0.6 gather_fusion.7
  92.9 4.8 %fusion.174 = bf16[16,128,128]{2,1,0:T(8,128)(2,1)S(1)} fusion(s32[16,128,128]{2,1,0:T(8,128)S(1)} %copy.53, f32[128]{0:T(128)} %get-tuple-element.1175, s32[128]{0:T(128)S(1)} %get-tuple-element.1174, pred[128]{0:T(512)(128)(4,1)} %get-tuple-element.1176), kind=kLoop, calls=%fused_computation.49.clone.1 | loop fusion | flops 3407872 | bytes 1574016 | tf_op jit(solution)/shard_map/convert_element_type | solution.py:29
  97.7 0.6 gather_fusion.8
  99.3 0.7 gather_fusion.6
  100.0 0.7 gather_fusion.9
  100.8 0.7 copy-done.6
  101.4 1.1 scatter_fusion.1
  103.3 1.2 fusion.171
  104.4 0.6 gather_fusion.5
  105.1 0.6 fusion.169
  105.7 0.6 gather_fusion
  106.3 0.5 multiply_reduce_fusion.13
  106.9 0.6 copy-done.8
  107.6 1.1 scatter_fusion
  108.7 0.6 copy-done.11
  109.4 0.6 copy-done.1
  110.0 0.6 fusion.102
  110.8 0.6 copy-done.24
  111.5 0.7 dynamic-slice
  112.1 0.6 dynamic-slice.2
  112.7 5.0 %all-reduce.1 = f32[2,128,8]{1,2,0:T(8,128)S(1)} all-reduce(f32[2,128,8]{1,2,0:T(8,128)S(1)} %get-tuple-element.391), channel_id=3, replica_groups=mesh['row'=2,'col'=16] {'row'}, use_global_device_ids=true, to_apply=%region_11.13.clone | all-reduce | flops 2048 | bytes 16384
  117.7 95.3 %all-reduce.8.cloned.1.call-done = f32[16,128,8]{1,2,0:T(8,128)} async-done(((f32[16,128,8]{1,2,0:T(8,128)}), f32[16,128,8]{1,2,0:T(8,128)}) %all-reduce.8.cloned.1.call-update) | async-done | bytes 65552
  212.9 1.9 multiply_convert_fusion
  214.9 22.1 %all_gather.31 = bf16[2048,8]{0,1:T(8,128)(2,1)S(1)} all-gather(bf16[128,8]{0,1:T(8,128)(2,1)S(1)} %get-tuple-element.780), channel_id=1, replica_groups=mesh['row'=2,'col'=16] {'col'}, dimensions={0}, use_global_device_ids=true | all-gather | bytes 34816 | tf_op jit(solution)/shard_map/all_gather | solution.py:167
  236.9 4.3 %all_gather.30 = bf16[256,8]{0,1:T(8,128)(2,1)S(1)} all-gather(bf16[128,8]{0,1:T(8,128)(2,1)S(1)} %get-tuple-element.780), channel_id=1, replica_groups=mesh['row'=2,'col'=16] {'row'}, dimensions={0}, use_global_device_ids=true | all-gather | bytes 6144 | tf_op jit(solution)/shard_map/all_gather | solution.py:170
  241.2 13.1 %while.33 = (s32[]{:T(128)}, f32[16,128,8]{1,2,0:T(8,128)S(1)}, f32[2,128,8]{1,2,0:T(8,128)S(1)}, s32[]{:T(128)}, s32[32]{0:T(128)S(1)}, /*index=5*/bf16[16,128,...) while((s32[]{:T(128)}, f32[16,128,8]{1,2,0:T(8,128)S(1)}, ...), condition=%wide.region_19.21_spmd.clone.clone, body=%wide.region_14.20_spmd.clone.clone.sunk | while | flops 204562752 | bytes 11597213 | solution.py:105
  241.6 0.6 gather_fusion.12
  242.2 0.6 gather_fusion.13
  242.9 0.6 gather_fusion.11
  243.5 0.6 gather_fusion.14
  244.8 0.6 gather_fusion.17
  245.7 0.7 gather_fusion.18
  247.2 0.7 gather_fusion.16
  248.0 0.7 gather_fusion.19
  248.8 1.1 scatter_fusion.3
  250.0 0.7 gather_fusion.15
  250.7 0.6 fusion.182
  251.3 0.6 gather_fusion.10
  252.5 1.1 scatter_fusion.2
  253.6 0.7 copy-done.15
  254.3 0.6 copy-done
  255.0 5.0 %all-reduce.3 = f32[2,128,8]{1,2,0:T(8,128)S(1)} all-reduce(f32[2,128,8]{1,2,0:T(8,128)S(1)} %get-tuple-element.393), channel_id=5, replica_groups=mesh['row'=2,'col'=16] {'row'}, use_global_device_ids=true, to_apply=%region_21.23.clone | all-reduce | flops 2048 | bytes 16384
  260.0 88.6 %all-reduce.10.cloned.1.call-done = f32[16,128,8]{1,2,0:T(8,128)} async-done(((f32[16,128,8]{1,2,0:T(8,128)}), f32[16,128,8]{1,2,0:T(8,128)}) %all-reduce.10.cloned.1.call-update) | async-done | bytes 65552
  348.5 2.1 multiply_reduce_fusion.6
  350.6 41.9 %all-reduce.4 = (f32[8]{0:T(128)S(1)}, f32[8]{0:T(128)S(1)}, f32[8]{0:T(128)S(1)}) all-reduce(f32[8]{0:T(128)S(1)} %get-tuple-element.680, f32[8]{0:T(128)S(1)} %get-tuple-element.679, f32[8]{0:T(128)S(1)} %get-tuple-element.678), channel_id=1, replica_groups=mesh['row'=2,'col'=16] {'row','col'}, use_global_device_ids=true, to_apply=%region_13.15 | all-reduce | flops 24 | bytes 192 | tf_op jit(solution)/shard_map/psum | solution.py:181
  392.5 0.5 multiply_multiply_fusion
  393.0 2.6 multiply_subtract_fusion
  (120 shorter events, 8.2 us)
Async XLA Ops:
  7.2 29.4 %copy-start.4 = (bf16[128,128]{1,0:T(8,128)(2,1)S(1)}, bf16[128,128]{1,0:T(8,128)(2,1)}, u32[]{:S(2)}) copy-start(bf16[128,128]{1,0:T(8,128)(2,1)} %param.10) | copy-start | bytes 98308
  7.2 205.8 %all-reduce.8.cloned.1.call-start = ((), (), s32[]{:S(2)}) async-start(), calls=%async_computation | async-start | bytes 131072
  8.7 0.7 copy-start.21
  55.3 4.7 %copy-start.20 = (s32[128,8]{0,1:T(8,128)S(1)}, s32[128,8]{0,1:T(8,128)}, u32[]{:S(2)}) copy-start(s32[128,8]{0,1:T(8,128)} %param.12) | copy-start | bytes 12292
  87.1 5.0 %copy-start.2 = (s32[2048,8]{0,1:T(8,128)}, s32[2048,8]{0,1:T(8,128)S(1)}, u32[]{:S(2)}) copy-start(s32[2048,8]{0,1:T(8,128)S(1)} %get-tuple-element.1183) | copy-start | bytes 196612 | tf_op jit(solution)/shard_map/while
  87.2 5.7 %copy-start.9 = (s32[128]{0:T(128)}, s32[128]{0:T(128)S(1)}, u32[]{:S(2)}) copy-start(s32[128]{0:T(128)S(1)} %get-tuple-element.1174) | copy-start | bytes 1540 | tf_op jit(solution)/shard_map/while
  87.2 11.6 %copy-start.12 = (pred[16]{0:T(512)(128)(4,1)}, pred[16]{0:T(512)(128)(4,1)S(1)}, u32[]{:S(2)}) copy-start(pred[16]{0:T(512)(128)(4,1)S(1)} %get-tuple-element.1186) | copy-start | bytes 52 | tf_op jit(solution)/shard_map/while
  87.2 11.6 %copy-start.16 = (pred[2]{0:T(512)(128)(4,1)}, pred[2]{0:T(512)(128)(4,1)S(1)}, u32[]{:S(2)}) copy-start(pred[2]{0:T(512)(128)(4,1)S(1)} %get-tuple-element.1185) | copy-start | bytes 10 | tf_op jit(solution)/shard_map/while
  87.3 0.6 copy-start.5
  89.2 0.5 copy-start.7
  100.8 0.7 copy-start.6
  102.7 0.6 copy-start.10
  106.9 0.7 copy-start.8
  107.6 1.1 copy-start.3
  108.7 0.6 copy-start.11
  108.7 0.6 copy-start.13
  108.7 0.7 copy-start.17
  109.4 0.6 copy-start.1
  110.0 238.5 %all-reduce.10.cloned.1.call-start = ((), (), s32[]{:S(2)}) async-start(), calls=%async_computation.1 | async-start | bytes 131072
  110.8 0.7 copy-start.24
  111.5 0.7 copy-start.23
  241.4 5.3 %copy-start.14 = (pred[16]{0:T(512)(128)(4,1)}, pred[16]{0:T(512)(128)(4,1)S(1)}, u32[]{:S(2)}) copy-start(pred[16]{0:T(512)(128)(4,1)S(1)} %get-tuple-element.1264) | copy-start | bytes 52 | tf_op jit(solution)/shard_map/while
  241.5 5.3 %copy-start.18 = (pred[2]{0:T(512)(128)(4,1)}, pred[2]{0:T(512)(128)(4,1)S(1)}, u32[]{:S(2)}) copy-start(pred[2]{0:T(512)(128)(4,1)S(1)} %get-tuple-element.1263) | copy-start | bytes 10 | tf_op jit(solution)/shard_map/while
  253.6 0.7 copy-start.15
  253.6 0.7 copy-start.19
  254.3 0.6 copy-start
  254.3 0.7 copy-start.22
Sparse Core Ops, SparseCore 0:
  110.1 102.7 all-reduce.7
  255.1 93.4 all-reduce.9
where the time goes:
time: 403 us; the launch traced here: 402 us
  waiting for transfers between devices  184 us (46%)
  blocking collectives  152 us (38%)
  local copies, waits for them, and re-layouts  24.1 us (6%)
  other arithmetic  23.8 us (6%)
  between operations  14.8 us (4%)
    unnamed x4, waiting for transfers between devices  184 us
    psum x1, blocking collectives, on_device(): lax.psum((jnp.sum(right_side * right_side, axis=0), jnp.sum(right_side *...  41.9 us
    all_gather x1, blocking collectives, on_device(): lax.all_gather(logged_actions, 'col', axis=0, tiled=True)  23 us
    all_gather x1, blocking collectives, on_device(): lax.all_gather(right_low, 'col', axis=0, tiled=True)  22.1 us
    all_gather x1, blocking collectives, on_device(): lax.all_gather(policy_actions, 'col', axis=0, tiled=True)  19.1 us
    all_gather x1, blocking collectives, on_device(): lax.all_gather(contexts, 'col', axis=0, tiled=True)  18.7 us
    unnamed x2, blocking collectives  9.97 us
    convert_element_type x8, other arithmetic, action_features(): jnp.where(levels == 0, constant_term, wave_terms).astype(jnp.bfloat16)  8.19 us
  transfers between devices with their start and end apart: 2, of which 2 were waited for; matrix products, arithmetic and copies ran while one was open for 0% of the time, Pallas kernels for 0%

commit v1 on v0

v1 whole, which is shorter than its diff:
```python
import functools
import math

import jax
import jax.numpy as jnp
from jax import lax
from jax.experimental import pallas as pl
from jax.experimental.pallas import tpu as pltpu
from jax.sharding import PartitionSpec as P

MESH = pl.DeviceIdType.MESH
F32 = jnp.float32
BF16 = jnp.bfloat16

NPOL = 8
NACT = 16
CATALOG = 131042
RIDGE = 0.1
STRIDE = 1009
PHASE = 0.37
TWO_PI = 2.0 * math.pi
META = 32


def loop(low, high, body):
    if isinstance(low, int) and isinstance(high, int) and high - low <= 4:
        for step in range(low, high):
            body(step)
    else:

        def wrapped(step, carried):
            body(step)
            return carried

        lax.fori_loop(low, high, wrapped, 0)


def cosine(turned, phase):
    whole = jnp.floor(turned.astype(F32) * (1.0 / CATALOG) + 0.5).astype(jnp.int32)
    rest = (turned - whole * CATALOG).astype(F32)
    turns = rest * (1.0 / CATALOG) + phase / TWO_PI
    turns = turns - jnp.floor(turns + 0.5)
    angle = TWO_PI * (0.25 - jnp.abs(turns))
    square = angle * angle
    series = -1.0 / 39916800.0
    for term in (362880.0, -5040.0, 120.0, -6.0, 1.0):
        series = series * square + 1.0 / term
    return series * angle


def features(chosen):
    twice = 2.0 * cosine(chosen * STRIDE, PHASE)
    before = cosine(chosen, 0.0)
    now = cosine(chosen * (1 + STRIDE), PHASE)
    scale = math.sqrt(2.0 / NACT)
    out = [jnp.full(chosen.shape, 1.0 / math.sqrt(NACT), F32)]
    for level in range(1, NACT):
        out.append(scale * now)
        before, now = now, twice * now - before
    return out


def rounded(parts):
    return jnp.concatenate(parts, axis=0).astype(BF16)


def nt_dot(left, right):
    return lax.dot_general(left, right, (((1,), (1,)), ((), ())), preferred_element_type=F32)


def kernel(
    sizes,
    ctx_ref,
    logged_ref,
    policy_ref,
    reward_ref,
    weights_ref,
    residual_ref,
    values_ref,
    blocks,
    sides,
    grams,
    logged_feat,
    total,
    square_part,
    slots,
    block_send,
    block_recv,
    side_send,
    side_recv,
    sum_send,
    sum_recv,
):
    rows_n, depth, width = sizes
    half = rows_n * width * depth
    count = 2 * half
    rows, dims = ctx_ref.shape
    x = lax.axis_index("row")
    col = lax.axis_index("col")
    core = col % 2
    y = (col // 2) % width
    z = col // (2 * width)
    if rows_n == width:
        n1 = n2 = width
    else:
        n1 = width + core * (rows_n - width)
        n2 = rows_n + core * (width - rows_n)
    i1 = y + core * (x - y)
    i2 = x + core * (y - x)
    own_half = core * half
    own_group = i2 * n1 + i1
    me = own_half + own_group * depth + z

    def device(first, second, at_z, at_core):
        at_x = second + core * (first - second)
        at_y = first + core * (second - first)
        return (at_x, (at_z * width + at_y) * 2 + at_core)

    def z_peer(step):
        return device(i1, i2, (z + step) % depth, core)

    def first_peer(step):
        return device((i1 + step) % n1, i2, z, core)

    def second_peer(step):
        return device(i1, (i2 + step) % n2, z, core)

    core_peer = (x, (z * width + y) * 2 + 1 - core)

    barrier = pltpu.get_barrier_semaphore()

    def greet(peer):
        pl.semaphore_signal(barrier, inc=1, device_id=peer, device_id_type=MESH)

    loop(1, depth, lambda step: greet(z_peer(step)))
    loop(1, n1, lambda step: greet(first_peer(step)))
    loop(1, n2, lambda step: greet(second_peer(step)))
    greet(core_peer)

    own = ctx_ref[...]
    own_wide = own.astype(F32)
    own_squares = jnp.sum(own_wide * own_wide, axis=1, keepdims=True) * (1.0 / dims)
    square_part[...] = jnp.zeros_like(square_part)
    square_part[:, 0:NPOL] = policy_ref[...].astype(F32)
    square_part[:, NPOL : NPOL + 1] = own_squares
    turned = square_part[...].T
    chosen = turned[0:NPOL]
    squares_row = turned[NPOL : NPOL + 1]
    logged = logged_ref[...].astype(F32)

    def pieces(value):
        high = jnp.floor(value * (1.0 / 512.0) + 0.5)
        return high, value - 512.0 * high

    policy_high, policy_low = pieces(chosen)
    logged_high, logged_low = pieces(logged)
    square_1 = squares_row.astype(BF16).astype(F32)
    square_2 = (squares_row - square_1).astype(BF16).astype(F32)
    square_3 = squares_row - square_1 - square_2
    meta = jnp.concatenate(
        [
            policy_high,
            policy_low,
            jnp.broadcast_to(logged_high, (8, rows)),
            logged_low,
            square_1,
            square_2,
            square_3,
            jnp.zeros((4, rows), F32),
        ],
        axis=0,
    )
    blocks[me, 0:rows, :] = own
    blocks[me, rows : rows + META, :] = meta.astype(BF16)
    own_feat = [
        part.astype(BF16).astype(F32)
        for part in features(jnp.broadcast_to(logged_ref[...], (NPOL, rows)))
    ]

    peers = (depth - 1) + (n1 - 1) + (n2 - 1) + 1
    pl.semaphore_wait(barrier, peers)

    def spread(buffer, send_sem, recv_sem, use_group):
        def copy(index, peer):
            return pltpu.make_async_remote_copy(
                src_ref=buffer.at[index],
                dst_ref=buffer.at[index],
                send_sem=send_sem,
                recv_sem=recv_sem.at[index],
                device_id=peer,
                device_id_type=MESH,
            )

        def to_first(index):
            loop(1, n1, lambda step: copy(index, first_peer(step)).start())

        def to_second(index):
            loop(1, n2, lambda step: copy(index, second_peer(step)).start())

        def to_core(index):
            copy(index, core_peer).start()

        def arrive(index):
            copy(index, core_peer).wait_recv()

        loop(1, depth, lambda step: copy(me, z_peer(step)).start())
        to_first(me)
        to_second(me)
        to_core(me)

        def from_z(step):
            index = own_half + own_group * depth + (z + step) % depth
            arrive(index)
            to_first(index)
            to_second(index)
            to_core(index)

        loop(1, depth, from_z)
        use_group(own_half // depth + own_group)

        def from_first(step):
            group = i2 * n1 + (i1 + step) % n1

            def one(place):
                index = own_half + group * depth + place
                arrive(index)
                to_second(index)
                to_core(index)

            loop(0, depth, one)
            use_group(own_half // depth + group)

        loop(1, n1, from_first)

        def from_second(step):
            def inner(first):
                group = ((i2 + step) % n2) * n1 + first

                def one(place):
                    index = own_half + group * depth + place
                    arrive(index)
                    to_core(index)

                loop(0, depth, one)
                use_group(own_half // depth + group)

            loop(0, n1, inner)

        loop(1, n2, from_second)

        def from_core(group):
            other = (1 - core) * half
            loop(0, depth, lambda place: arrive(other + group * depth + place))
            use_group(other // depth + group)

        lax.fori_loop(0, half // depth, lambda g, c: (from_core(g), c)[1], 0)

    def finish(buffer, copies, send_sem, recv_sem):
        everything = buffer.at[pl.ds(0, copies)]
        pltpu.make_async_remote_copy(
            src_ref=everything,
            dst_ref=everything,
            send_sem=send_sem,
            recv_sem=recv_sem.at[0],
            device_id=core_peer,
            device_id_type=MESH,
        ).wait_send()

    total[...] = jnp.zeros_like(total)
    wide = depth * rows

    def first_pass(group):
        base = group * depth
        metas = [blocks[base + k, rows : rows + META, :].astype(F32) for k in range(depth)]
        meta_all = jnp.concatenate(metas, axis=1)
        policy = (meta_all[0:8] * 512.0 + meta_all[8:16]).astype(jnp.int32)
        shown = (meta_all[16:17] * 512.0 + meta_all[24:25]).astype(jnp.int32)
        squares = meta_all[25:26] + meta_all[26:27] + meta_all[27:28]
        policy_feat = rounded(features(policy))
        logged_feat[group] = rounded(features(jnp.broadcast_to(shown, (NPOL, wide))))
        others = jnp.concatenate([blocks[base + k, 0:rows, :] for k in range(depth)], axis=0)
        inner = nt_dot(own, others)
        gram = jnp.exp(inner * (2.0 / dims) - own_squares - squares).astype(BF16)
        grams[group] = gram
        total[...] += nt_dot(policy_feat, gram)

    spread(blocks, block_send, block_recv, first_pass)

    factor = NACT / (rows * count)

    def select():
        value = total[...]
        out = own_feat[0] * value[0:NPOL]
        for level in range(1, NACT):
            out += own_feat[level] * value[level * NPOL : (level + 1) * NPOL]
        return factor * out

    right_side = select()
    sides[me] = right_side
    total[...] = jnp.zeros_like(total)

    def second_pass(group):
        base = group * depth
        low = jnp.concatenate([sides[base + k] for k in range(depth)], axis=1)
        low = low.astype(BF16).astype(F32)
        feat = logged_feat[group].astype(F32)
        matched = (feat * jnp.concatenate([low] * NACT, axis=0)).astype(BF16)
        total[...] += nt_dot(matched, grams[group])

    spread(sides, side_send, side_recv, second_pass)
    image = select() + RIDGE * right_side

    lane = lax.broadcasted_iota(jnp.int32, (NPOL, rows), 1)
    sub = lax.broadcasted_iota(jnp.int32, (NPOL, rows), 0)

    def to_row(value, offset):
        column = jnp.sum(value, axis=1, keepdims=True)
        return jnp.sum(jnp.where(lane == sub + offset, column, 0.0), axis=0, keepdims=True)

    partial = (
        to_row(right_side * right_side, 0)
        + to_row(right_side * image, NPOL)
        + to_row(reward_ref[...] * right_side, 2 * NPOL)
    )

    most = max(rows_n, width)

    def all_sum(value, base, at, size, peer_of):
        slots[base + at] = value

        def copy(source, peer):
            return pltpu.make_async_remote_copy(
                src_ref=slots.at[base + source],
                dst_ref=slots.at[base + source],
                send_sem=sum_send,
                recv_sem=sum_recv.at[base + source],
                device_id=peer,
                device_id_type=MESH,
            )

        loop(1, size, lambda step: copy(at, peer_of(step)).start())
        loop(1, size, lambda step: copy((at + step) % size, core_peer).wait_recv())
        if isinstance(size, int):
            out = slots[base]
            for place in range(1, size):
                out = out + slots[base + place]
            return out
        return lax.fori_loop(
            0, size, lambda place, out: out + slots[base + place], jnp.zeros_like(value)
        )

    partial = all_sum(partial, 0, z, depth, z_peer)
    partial = all_sum(partial, depth, i1, n1, first_peer)
    partial = all_sum(partial, depth + most, i2, n2, second_peer)
    partial = all_sum(partial, depth + 2 * most, core, 2, lambda step: core_peer)

    def to_column(offset):
        spread_row = jnp.broadcast_to(partial, (NPOL, rows))
        return jnp.sum(jnp.where(lane == sub + offset, spread_row, 0.0), axis=1, keepdims=True)

    alpha = to_column(0) / to_column(NPOL)
    values_column = alpha * to_column(2 * NPOL) * (1.0 / (rows * count))
    values_ref[...] = jnp.sum(jnp.where(lane == sub, values_column, 0.0), axis=0, keepdims=True)
    square_part[0:NPOL, :] = alpha * right_side
    square_part[NPOL : 2 * NPOL, :] = right_side - alpha * image
    results = square_part[...].T
    weights_ref[...] = results[:, 0:NPOL]
    residual_ref[...] = results[:, NPOL : 2 * NPOL]

    finish(blocks, count - 1, block_send, block_recv)
    finish(sides, count - 1, side_send, side_recv)
    finish(slots, depth + rows_n + width - 2, sum_send, sum_recv)


def on_device(sizes, contexts, logged_actions, policy_actions, rewards):
    rows_n, depth, width = sizes
    rows, dims = contexts.shape
    count = 2 * rows_n * width * depth
    groups = count // depth
    most = max(rows_n, width)
    vmem = pl.BlockSpec(memory_space=pltpu.VMEM)
    weights, residual, values = pl.pallas_call(
        functools.partial(kernel, sizes),
        out_shape=(
            jax.ShapeDtypeStruct((rows, NPOL), F32),
            jax.ShapeDtypeStruct((rows, NPOL), F32),
            jax.ShapeDtypeStruct((1, rows), F32),
        ),
        in_specs=[vmem] * 4,
        out_specs=(vmem,) * 3,
        scratch_shapes=[
            pltpu.VMEM((count, rows + META, dims), BF16),
            pltpu.VMEM((count, NPOL, rows), F32),
            pltpu.VMEM((groups, rows, depth * rows), BF16),
            pltpu.VMEM((groups, NPOL * NACT, depth * rows), BF16),
            pltpu.VMEM((NPOL * NACT, rows), F32),
            pltpu.VMEM((rows, dims), F32),
            pltpu.VMEM((depth + 2 * most + 2, 1, rows), F32),
            pltpu.SemaphoreType.DMA,
            pltpu.SemaphoreType.DMA((count,)),
            pltpu.SemaphoreType.DMA,
            pltpu.SemaphoreType.DMA((count,)),
            pltpu.SemaphoreType.DMA,
            pltpu.SemaphoreType.DMA((depth + 2 * most + 2,)),
        ],
        compiler_params=pltpu.CompilerParams(
            collective_id=0, has_side_effects=True, vmem_limit_bytes=48 * 1024 * 1024
        ),
    )(contexts, logged_actions.reshape(1, rows), policy_actions, rewards.reshape(1, rows))
    return weights, residual, values[0, 0:NPOL]


def solution(mesh):
    rows_n, cols = mesh.shape["row"], mesh.shape["col"]
    depth = 4 if (cols // 2) % 4 == 0 else 1
    sizes = (rows_n, depth, cols // 2 // depth)
    placed = (
        P(("row", "col"), None),
        P(("row", "col")),
        P(("row", "col"), None),
        P(("row", "col")),
    )
    return jax.shard_map(
        functools.partial(on_device, sizes),
        mesh=mesh,
        in_specs=placed,
        out_specs=(P(("row", "col"), None), P(("row", "col"), None), P()),
        check_vma=False,
    )
```

time: 403 us -> 45.3 us (0.11)
  waiting for transfers between devices: 184 us -> 0 us
  blocking collectives: 152 us -> 0 us
  Pallas kernels: 0 us -> 41.7 us
  other arithmetic: 23.8 us -> 0 us
  local copies, waits for them, and re-layouts: 24.1 us -> 2.65 us
  between operations: 14.8 us -> 0.68 us
    unnamed x4 -> x0, waiting for transfers between devices: 184 us -> none
    all_gather x8 -> x0, blocking collectives: 100 us -> none  [the longest x1 23 us: on_device(): lax.all_gather(logged_actions, 'col', axis=0, tiled=True)]
    psum x1 -> x0, blocking collectives: 41.9 us -> none  [on_device(): lax.psum((jnp.sum(right_side * right_side, axis=0), jnp.sum(right_side *...]
    pallas_call x0 -> x1, Pallas kernels: none -> 41.7 us  [on_device(): pl.pallas_call(functools.partial(kernel, sizes), out_shape=(jax.ShapeDtyp...]
    gather x20 -> x0, local copies, waits for them, and re-layouts: 12.4 us -> none  [the longest x2 1.32 us: advance(): jnp.take(flat_diagonal, picked)]
    convert_element_type x15 -> x0, other arithmetic: 10.2 us -> none  [the longest x8 8.19 us: action_features(): jnp.where(levels == 0, constant_term, wave_terms).astype(jnp.bfloat16)]
    unnamed x2 -> x0, blocking collectives: 9.97 us -> none
    while x35 -> x0, local copies, waits for them, and re-layouts: 4.43 us -> none
  transfers between devices with their start and end apart: 2 -> 0, of which waited for: 2 -> 0; matrix products, arithmetic and copies ran while one was open for 0% -> 0% of each run, Pallas kernels for 0% -> 0%
where the time goes in v1:
time: 45.3 us; the launch traced here: 45 us
  Pallas kernels  41.7 us (92%)
  local copies, waits for them, and re-layouts  2.65 us (6%)
  between operations  0.68 us (2%)
    pallas_call x1, Pallas kernels, on_device(): pl.pallas_call(functools.partial(kernel, sizes), out_shape=(jax.ShapeDtyp...  41.7 us
    unnamed x9, local copies, waits for them, and re-layouts  2.14 us

profile of v1, /device:TPU:0, one launch (start us, length us, event | category | flops | bytes accessed | tf_op | source)
XLA Modules:
  0.0 45.0 jit_solution(10753248253345990748)
XLA Ops:
  0.6 0.0 copy-start
  0.6 0.0 copy-start.1
  0.7 0.0 copy-start.2
  0.7 0.8 %copy.7.policy_ref = s32[128,8]{1,0:T(8,128)S(1)} copy(s32[128,8]{0,1:T(8,128)} %param.6) | data formatting | bytes 8192 | tf_op args[2]
  1.5 0.0 copy-done
  1.5 0.0 copy-done.1
  1.5 0.0 copy-done.2
  1.5 41.7 %shard_map.67 = (f32[128,8]{1,0:T(8,128)S(1)}, f32[128,8]{1,0:T(8,128)S(1)}, f32[1,128]{1,0:T(1,128)S(1)}) custom-call(bf16[128,128]{1,0:T(8,128)(2,1)S(1)} %copy-done, s32[1,128]{1,0:T(1,128)S(1)} %bitcast.4, s32[128,8]{1,0:T(8,128)S(1)} %copy.7.policy_ref, f32[1,128]{1,0:T(1,128)S(1)} %bitcast.5), custom_call_target="tpu_custom_call" | custom-call | tf_op jit(solution)/shard_map/pallas_call | solution.py:382
  43.2 0.7 %copy.8 = f32[128,8]{0,1:T(8,128)} copy(f32[128,8]{1,0:T(8,128)S(1)} %get-tuple-element.9) | data formatting | bytes 8192
  43.9 0.5 %slice_bitcast_fusion = f32[8]{0:T(128)} fusion(f32[1,128]{1,0:T(1,128)S(1)} %get-tuple-element.8), kind=kLoop, calls=%fused_computation | loop fusion | bytes 64 | tf_op jit(solution)/shard_map/squeeze | solution.py:410
  44.4 0.7 %copy.9 = f32[128,8]{0,1:T(8,128)} copy(f32[128,8]{1,0:T(8,128)S(1)} %get-tuple-element.10) | data formatting | bytes 8192
Async XLA Ops:
  0.6 0.8 %copy-start = (bf16[128,128]{1,0:T(8,128)(2,1)S(1)}, bf16[128,128]{1,0:T(8,128)(2,1)}, u32[]{:S(2)}) copy-start(bf16[128,128]{1,0:T(8,128)(2,1)} %ctx_ref.1) | copy-start | bytes 98308
  0.6 0.8 %copy-start.1 = (s32[128]{0:T(128)S(1)}, s32[128]{0:T(128)}, u32[]{:S(2)}) copy-start(s32[128]{0:T(128)} %param.5) | copy-start | bytes 1540
  0.7 0.8 %copy-start.2 = (f32[128]{0:T(128)S(1)}, f32[128]{0:T(128)}, u32[]{:S(2)}) copy-start(f32[128]{0:T(128)} %param.7) | copy-start | bytes 1540

commit v2 on v1

v2 whole, which is shorter than its diff:
```python
import functools
import math

import jax
import jax.numpy as jnp
from jax import lax
from jax.experimental import pallas as pl
from jax.experimental.pallas import tpu as pltpu
from jax.sharding import PartitionSpec as P

MESH = pl.DeviceIdType.MESH
F32 = jnp.float32
BF16 = jnp.bfloat16

NPOL = 8
NACT = 16
CATALOG = 131042
RIDGE = 0.1
STRIDE = 1009
PHASE = 0.37
TWO_PI = 2.0 * math.pi
META = 32


def loop(low, high, body):
    if isinstance(low, int) and isinstance(high, int) and high - low <= 4:
        for step in range(low, high):
            body(step)
    else:

        def wrapped(step, carried):
            body(step)
            return carried

        lax.fori_loop(low, high, wrapped, 0)


def cosine(turned, phase):
    whole = jnp.floor(turned.astype(F32) * (1.0 / CATALOG) + 0.5).astype(jnp.int32)
    rest = (turned - whole * CATALOG).astype(F32)
    turns = rest * (1.0 / CATALOG) + phase / TWO_PI
    turns = turns - jnp.floor(turns + 0.5)
    angle = TWO_PI * (0.25 - jnp.abs(turns))
    square = angle * angle
    series = -1.0 / 39916800.0
    for term in (362880.0, -5040.0, 120.0, -6.0, 1.0):
        series = series * square + 1.0 / term
    return series * angle


def features(chosen):
    twice = 2.0 * cosine(chosen * STRIDE, PHASE)
    before = cosine(chosen, 0.0)
    now = cosine(chosen * (1 + STRIDE), PHASE)
    scale = math.sqrt(2.0 / NACT)
    out = [jnp.full(chosen.shape, 1.0 / math.sqrt(NACT), F32)]
    for level in range(1, NACT):
        out.append(scale * now)
        before, now = now, twice * now - before
    return out


def rounded(parts):
    return jnp.concatenate(parts, axis=0).astype(BF16)


def nt_dot(left, right):
    return lax.dot_general(left, right, (((1,), (1,)), ((), ())), preferred_element_type=F32)


def kernel(
    sizes,
    ctx_ref,
    logged_ref,
    policy_ref,
    reward_ref,
    results_ref,
    blocks,
    sides,
    grams,
    logged_feat,
    total,
    logged_own,
    policy_own,
    reward_own,
    near_sums,
    plane_sums,
    load_sem,
    block_send,
    block_recv,
    side_send,
    side_recv,
    side_recv_plane,
    sum_send,
    sum_recv,
    sum_recv_plane,
):
    rows_n, depth, width = sizes
    half_groups = rows_n * width
    half = half_groups * depth
    plane = 2 * half_groups
    count = 2 * half
    rows, dims = ctx_ref.shape
    x = lax.axis_index("row")
    col = lax.axis_index("col")
    core = col % 2
    y = (col // 2) % width
    z = col // (2 * width)

    def inner_size(at_core):
        return width if rows_n == width else width + at_core * (rows_n - width)

    n1 = inner_size(core)
    n2 = inner_size(1 - core)
    i1 = y + core * (x - y)
    i2 = x + core * (y - x)
    own_half = core * half_groups
    own_group = own_half + i2 * n1 + i1
    me = own_group * depth + z

    def device(first, second, at_z, at_core):
        at_x = second + at_core * (first - second)
        at_y = first + at_core * (second - first)
        return (at_x, (at_z * width + at_y) * 2 + at_core)

    def z_peer(step):
        return device(i1, i2, (z + step) % depth, core)

    def first_peer(step):
        return device((i1 + step) % n1, i2, z, core)

    def second_peer(step):
        return device(i1, (i2 + step) % n2, z, core)

    def plane_peer(step):
        group = (own_group + step) % plane
        at_core = group // half_groups
        place = group % half_groups
        inside = inner_size(at_core)
        return device(place % inside, place // inside, z, at_core)

    core_peer = (x, (z * width + y) * 2 + 1 - core)

    barrier = pltpu.get_barrier_semaphore()

    def greet(peer):
        pl.semaphore_signal(barrier, inc=1, device_id=peer, device_id_type=MESH)

    loop(1, depth, lambda step: greet(z_peer(step)))
    loop(1, plane, lambda step: greet(plane_peer(step)))

    loads = [
        pltpu.make_async_copy(source, target, load_sem.at[place])
        for place, (source, target) in enumerate(
            (
                (ctx_ref, blocks.at[me, pl.ds(0, rows)]),
                (logged_ref, logged_own),
                (policy_ref, policy_own),
                (reward_ref, reward_own),
            )
        )
    ]
    for load in loads:
        load.start()
    for load in loads:
        load.wait()

    own = blocks[me, 0:rows, :]
    own_wide = own.astype(F32)
    own_squares = jnp.sum(own_wide * own_wide, axis=1, keepdims=True) * (1.0 / dims)
    here = lax.broadcasted_iota(jnp.int32, (rows, rows), 0)
    there = lax.broadcasted_iota(jnp.int32, (rows, rows), 1)
    squares_row = jnp.sum(jnp.where(here == there, own_squares, 0.0), axis=0, keepdims=True)

    def pieces(value):
        high = jnp.floor(value * (1.0 / 512.0) + 0.5)
        return high, value - 512.0 * high

    policy_high, policy_low = pieces(policy_own[...].astype(F32))
    logged_high, logged_low = pieces(logged_own[...].astype(F32))
    square_1 = squares_row.astype(BF16).astype(F32)
    square_2 = (squares_row - square_1).astype(BF16).astype(F32)
    square_3 = squares_row - square_1 - square_2
    meta = jnp.concatenate(
        [
            policy_high,
            policy_low,
            jnp.broadcast_to(logged_high, (8, rows)),
            logged_low,
            square_1,
            square_2,
            square_3,
            jnp.zeros((4, rows), F32),
        ],
        axis=0,
    )
    blocks[me, rows : rows + META, :] = meta.astype(BF16)
    total[...] = jnp.zeros_like(total)
    pl.semaphore_wait(barrier, (depth - 1) + (plane - 1))

    def remote(source, send_sem, recv_sem, peer):
        return pltpu.make_async_remote_copy(
            src_ref=source,
            dst_ref=source,
            send_sem=send_sem,
            recv_sem=recv_sem,
            device_id=peer,
            device_id_type=MESH,
        )

    def block_copy(index, peer):
        return remote(blocks.at[index], block_send, block_recv.at[index], peer)

    def group_copy(group):
        start = group * depth
        return remote(blocks.at[pl.ds(start, depth)], block_send, block_recv.at[start], core_peer)

    def to_first(index):
        loop(1, n1, lambda step: block_copy(index, first_peer(step)).start())

    def to_second(index):
        loop(1, n2, lambda step: block_copy(index, second_peer(step)).start())

    wide = depth * rows

    def meta_of(group):
        base = group * depth
        return jnp.concatenate(
            [blocks[base + k, rows : rows + META, :].astype(F32) for k in range(depth)], axis=1
        )

    def first_pass(group):
        base = group * depth
        meta_all = meta_of(group)
        policy = (meta_all[0:8] * 512.0 + meta_all[8:16]).astype(jnp.int32)
        squares = meta_all[25:26] + meta_all[26:27] + meta_all[27:28]
        others = jnp.concatenate([blocks[base + k, 0:rows, :] for k in range(depth)], axis=0)
        inner = nt_dot(own, others)
        policy_feat = rounded(features(policy))
        gram = jnp.exp(inner * (2.0 / dims) - own_squares - squares).astype(BF16)
        grams[group] = gram
        total[...] += nt_dot(policy_feat, gram)

    def from_core(group):
        group_copy(group).wait_recv()
        first_pass(group)

    loop(1, depth, lambda step: block_copy(me, z_peer(step)).start())
    to_first(me)
    to_second(me)

    def from_z(step):
        index = own_group * depth + (z + step) % depth
        block_copy(index, core_peer).wait_recv()
        to_first(index)
        to_second(index)

    loop(1, depth, from_z)
    group_copy(own_group).start()
    first_pass(own_group)

    def first_group(step):
        return own_half + i2 * n1 + (i1 + step) % n1

    def second_group(step, first):
        return own_half + ((i2 + step) % n2) * n1 + first

    other_half = half_groups - own_half
    peer_own = other_half + i1 * n2 + i2

    def from_first(step):
        group = first_group(step)

        def one(place):
            index = group * depth + place
            block_copy(index, core_peer).wait_recv()
            to_second(index)

        loop(0, depth, one)
        group_copy(group).start()

    loop(1, n1, from_first)
    from_core(peer_own)
    loop(1, n1, lambda step: first_pass(first_group(step)))

    def from_second(step, first):
        group = second_group(step, first)
        loop(0, depth, lambda k: block_copy(group * depth + k, core_peer).wait_recv())
        group_copy(group).start()

    loop(1, n2, lambda step: loop(0, n1, lambda first: from_second(step, first)))
    loop(1, n2, lambda step: from_core(other_half + i1 * n2 + (i2 + step) % n2))
    loop(1, n2, lambda step: loop(0, n1, lambda first: first_pass(second_group(step, first))))
    loop(
        1,
        n1,
        lambda step: loop(
            0, n2, lambda second: from_core(other_half + ((i1 + step) % n1) * n2 + second)
        ),
    )

    factor = NACT / (rows * count)
    own_feat = [
        part.astype(BF16).astype(F32)
        for part in features(jnp.broadcast_to(logged_own[...], (NPOL, rows)))
    ]

    def select():
        value = total[...]
        out = own_feat[0] * value[0:NPOL]
        for level in range(1, NACT):
            out += own_feat[level] * value[level * NPOL : (level + 1) * NPOL]
        return factor * out

    right_side = select()
    sides[me] = right_side
    total[...] = jnp.zeros_like(total)

    def side_copy(index, peer):
        return remote(sides.at[index], side_send, side_recv.at[index], peer)

    def side_group(group, peer):
        rows_of = sides.at[pl.ds(group * depth, depth)]
        return remote(rows_of, side_send, side_recv_plane.at[group], peer)

    def show(group):
        meta_all = meta_of(group)
        shown = (meta_all[16:17] * 512.0 + meta_all[24:25]).astype(jnp.int32)
        logged_feat[group] = rounded(features(jnp.broadcast_to(shown, (NPOL, wide))))

    def second_pass(group):
        base = group * depth
        low = jnp.concatenate([sides[base + k] for k in range(depth)], axis=1)
        low = low.astype(BF16).astype(F32)
        feat = logged_feat[group].astype(F32)
        matched = (feat * jnp.concatenate([low] * NACT, axis=0)).astype(BF16)
        total[...] += nt_dot(matched, grams[group])

    loop(1, depth, lambda step: side_copy(me, z_peer(step)).start())
    loop(0, half_groups, show)
    loop(1, depth, lambda k: side_copy(own_group * depth + (z + k) % depth, core_peer).wait_recv())
    loop(1, plane, lambda step: side_group(own_group, plane_peer(step)).start())
    loop(half_groups, plane, show)
    second_pass(own_group)

    def from_plane(step):
        group = (own_group + step) % plane
        side_group(group, core_peer).wait_recv()
        second_pass(group)

    loop(1, plane, from_plane)
    image = select() + RIDGE * right_side

    lane = lax.broadcasted_iota(jnp.int32, (NPOL, rows), 1)
    sub = lax.broadcasted_iota(jnp.int32, (NPOL, rows), 0)

    def to_row(value, offset):
        column = jnp.sum(value, axis=1, keepdims=True)
        return jnp.sum(jnp.where(lane == sub + offset, column, 0.0), axis=0, keepdims=True)

    partial = (
        to_row(right_side * right_side, 0)
        + to_row(right_side * image, NPOL)
        + to_row(reward_own[...] * right_side, 2 * NPOL)
    )

    def all_sum(value, slots, recv, at, size, peer_of):
        slots[at] = value
        loop(
            1,
            size,
            lambda step: remote(slots.at[at], sum_send, recv.at[at], peer_of(step)).start(),
        )

        def arrive(step):
            place = (at + step) % size
            remote(slots.at[place], sum_send, recv.at[place], core_peer).wait_recv()

        loop(1, size, arrive)
        return jnp.sum(slots[...], axis=0)

    partial = all_sum(partial, near_sums, sum_recv, z, depth, z_peer)
    partial = all_sum(partial, plane_sums, sum_recv_plane, own_group, plane, plane_peer)

    def to_column(offset):
        spread_row = jnp.broadcast_to(partial, (NPOL, rows))
        return jnp.sum(jnp.where(lane == sub + offset, spread_row, 0.0), axis=1, keepdims=True)

    alpha = to_column(0) / to_column(NPOL)
    values_column = alpha * to_column(2 * NPOL) * (1.0 / (rows * count))
    values_row = jnp.sum(jnp.where(lane == sub, values_column, 0.0), axis=0, keepdims=True)
    results_ref[0:NPOL] = alpha * right_side
    results_ref[NPOL : 2 * NPOL] = right_side - alpha * image
    results_ref[2 * NPOL :] = jnp.broadcast_to(values_row, (NPOL, rows))

    remote(
        blocks.at[pl.ds(0, count - 1)], block_send, block_recv.at[0], core_peer
    ).wait_send()
    remote(sides.at[pl.ds(0, count - 1)], side_send, side_recv.at[0], core_peer).wait_send()
    remote(
        near_sums.at[pl.ds(0, depth - 1)], sum_send, sum_recv.at[0], core_peer
    ).wait_send()
    remote(
        plane_sums.at[pl.ds(0, plane - 1)], sum_send, sum_recv_plane.at[0], core_peer
    ).wait_send()


def on_device(sizes, contexts, logged_actions, policy_actions, rewards):
    rows_n, depth, width = sizes
    rows, dims = contexts.shape
    plane = 2 * rows_n * width
    count = plane * depth
    vmem = pl.BlockSpec(memory_space=pltpu.VMEM)
    hbm = pl.BlockSpec(memory_space=pltpu.HBM)
    results = pl.pallas_call(
        functools.partial(kernel, sizes),
        out_shape=jax.ShapeDtypeStruct((3 * NPOL, rows), F32),
        in_specs=[hbm] * 4,
        out_specs=vmem,
        scratch_shapes=[
            pltpu.VMEM((count, rows + META, dims), BF16),
            pltpu.VMEM((count, NPOL, rows), F32),
            pltpu.VMEM((plane, rows, depth * rows), BF16),
            pltpu.VMEM((plane, NPOL * NACT, depth * rows), BF16),
            pltpu.VMEM((NPOL * NACT, rows), F32),
            pltpu.VMEM((1, rows), jnp.int32),
            pltpu.VMEM((NPOL, rows), jnp.int32),
            pltpu.VMEM((1, rows), F32),
            pltpu.VMEM((depth, 1, rows), F32),
            pltpu.VMEM((plane, 1, rows), F32),
            pltpu.SemaphoreType.DMA((4,)),
            pltpu.SemaphoreType.DMA,
            pltpu.SemaphoreType.DMA((count,)),
            pltpu.SemaphoreType.DMA,
            pltpu.SemaphoreType.DMA((count,)),
            pltpu.SemaphoreType.DMA((plane,)),
            pltpu.SemaphoreType.DMA,
            pltpu.SemaphoreType.DMA((depth,)),
            pltpu.SemaphoreType.DMA((plane,)),
        ],
        compiler_params=pltpu.CompilerParams(
            collective_id=0, has_side_effects=True, vmem_limit_bytes=60 * 1024 * 1024
        ),
    )(contexts, logged_actions.reshape(1, rows), policy_actions.T, rewards.reshape(1, rows))
    return results[0:NPOL].T, results[NPOL : 2 * NPOL].T, results[2 * NPOL, 0:NPOL]


def solution(mesh):
    rows_n, cols = mesh.shape["row"], mesh.shape["col"]
    depth = 4 if (cols // 2) % 4 == 0 else 1
    sizes = (rows_n, depth, cols // 2 // depth)
    placed = (
        P(("row", "col"), None),
        P(("row", "col")),
        P(("row", "col"), None),
        P(("row", "col")),
    )
    return jax.shard_map(
        functools.partial(on_device, sizes),
        mesh=mesh,
        in_specs=placed,
        out_specs=(P(("row", "col"), None), P(("row", "col"), None), P()),
        check_vma=False,
    )
```

time: 45.3 us -> 40.1 us (0.89)
  Pallas kernels: 41.7 us -> 36.7 us
    pallas_call x1, Pallas kernels: 41.7 us -> 36.7 us  [on_device(): pl.pallas_call(functools.partial(kernel, sizes), out_shape=jax.ShapeDtype...]
    unnamed x9 -> x0, local copies, waits for them, and re-layouts: 2.14 us -> none
    transpose x0 -> x1, local copies, waits for them, and re-layouts: none -> 1.28 us  [on_device(): results[NPOL:2 * NPOL]]
    squeeze x1, local copies, waits for them, and re-layouts: 0.51 us -> 1.19 us  [on_device(): results[2 * NPOL, 0:NPOL]]
where the time goes in v2:
time: 40.1 us; the launch traced here: 39.8 us
  Pallas kernels  36.7 us (92%)
  local copies, waits for them, and re-layouts  2.47 us (6%)
  between operations  0.64 us (2%)
    pallas_call x1, Pallas kernels, on_device(): pl.pallas_call(functools.partial(kernel, sizes), out_shape=jax.ShapeDtype...  36.7 us
    transpose x1, local copies, waits for them, and re-layouts, on_device(): results[NPOL:2 * NPOL]  1.28 us
    squeeze x1, local copies, waits for them, and re-layouts, on_device(): results[2 * NPOL, 0:NPOL]  1.19 us

profile of v2, /device:TPU:0, one launch (start us, length us, event | category | flops | bytes accessed | tf_op | source)
XLA Modules:
  0.0 39.8 jit_solution(3441137334371136976)
XLA Ops:
  0.6 36.7 %shard_map.67 = f32[24,128]{1,0:T(8,128)} custom-call(bf16[128,128]{1,0:T(8,128)(2,1)} %ctx_ref.1, s32[1,128]{1,0:T(1,128)} %bitcast.10, s32[8,128]{1,0:T(8,128)} %bitcast.9, f32[1,128]{1,0:T(1,128)} %bitcast.11), custom_call_target="tpu_custom_call" | custom-call | tf_op jit(solution)/shard_map/pallas_call | solution.py:415
  37.3 1.3 %slice_bitcast_fusion = (f32[128,8]{0,1:T(8,128)}, f32[128,8]{0,1:T(8,128)}) fusion(f32[24,128]{1,0:T(8,128)} %shard_map.67), kind=kLoop, calls=%fused_computation | loop fusion | bytes 16384 | tf_op jit(solution)/shard_map/transpose | solution.py:445
  38.6 1.2 %slice_bitcast_fusion.2 = f32[8]{0:T(128)} fusion(f32[24,128]{1,0:T(8,128)} %shard_map.67), kind=kLoop, calls=%fused_computation.2 | loop fusion | bytes 64 | tf_op jit(solution)/shard_map/squeeze | solution.py:445

commit v3 on v2

--- a/solution.py
+++ b/solution.py
@@ -76,6 +76,7 @@
     reward_ref,
     results_ref,
     blocks,
+    near,
     sides,
     grams,
     logged_feat,
@@ -88,9 +89,10 @@
     load_sem,
     block_send,
     block_recv,
+    near_send,
+    near_recv,
     side_send,
     side_recv,
-    side_recv_plane,
     sum_send,
     sum_recv,
     sum_recv_plane,
@@ -103,9 +105,9 @@
     rows, dims = ctx_ref.shape
     x = lax.axis_index("row")
     col = lax.axis_index("col")
-    core = col % 2
-    y = (col // 2) % width
-    z = col // (2 * width)
+    core = lax.rem(col, 2)
+    y = lax.rem(lax.div(col, 2), width)
+    z = lax.div(col, 2 * width)
 
     def inner_size(at_core):
         return width if rows_n == width else width + at_core * (rows_n - width)
@@ -124,20 +126,20 @@
         return (at_x, (at_z * width + at_y) * 2 + at_core)
 
     def z_peer(step):
-        return device(i1, i2, (z + step) % depth, core)
+        return device(i1, i2, lax.rem(z + step, depth), core)
 
     def first_peer(step):
-        return device((i1 + step) % n1, i2, z, core)
+        return device(lax.rem(i1 + step, n1), i2, z, core)
 
     def second_peer(step):
-        return device(i1, (i2 + step) % n2, z, core)
+        return device(i1, lax.rem(i2 + step, n2), z, core)
 
     def plane_peer(step):
-        group = (own_group + step) % plane
-        at_core = group // half_groups
-        place = group % half_groups
+        group = lax.rem(own_group + step, plane)
+        at_core = lax.div(group, half_groups)
+        place = lax.rem(group, half_groups)
         inside = inner_size(at_core)
-        return device(place % inside, place // inside, z, at_core)
+        return device(lax.rem(place, inside), lax.div(place, inside), z, at_core)
 
     core_peer = (x, (z * width + y) * 2 + 1 - core)
 
@@ -250,7 +252,7 @@
     to_second(me)
 
     def from_z(step):
-        index = own_group * depth + (z + step) % depth
+        index = own_group * depth + lax.rem(z + step, depth)
         block_copy(index, core_peer).wait_recv()
         to_first(index)
         to_second(index)
@@ -260,10 +262,12 @@
     first_pass(own_group)
 
     def first_group(step):
-        return own_half + i2 * n1 + (i1 + step) % n1
-
-    def second_group(step, first):
-        return own_half + ((i2 + step) % n2) * n1 + first
+        return own_half + i2 * n1 + lax.rem(i1 + step, n1)
+
+    def second_group(place):
+        step = 1 + lax.div(place, n1)
+        first = lax.rem(i1 + lax.rem(place, n1), n1)
+        return own_half + lax.rem(i2 + step, n2) * n1 + first
 
     other_half = half_groups - own_half
     peer_own = other_half + i1 * n2 + i2
@@ -279,25 +283,38 @@
         loop(0, depth, one)
         group_copy(group).start()
 
+    def peer_first(step):
+        return other_half + i1 * n2 + lax.rem(i2 + step, n2)
+
+    def peer_second(place):
+        step = 1 + lax.div(place, n2)
+        second = lax.rem(i2 + lax.rem(place, n2), n2)
+        return other_half + lax.rem(i1 + step, n1) * n2 + second
+
+    def from_second(place):
+        group = second_group(place)
+        loop(0, depth, lambda k: block_copy(group * depth + k, core_peer).wait_recv())
+        group_copy(group).start()
+
+    own_last = (n2 - 1) * n1
+    peer_last = (n1 - 1) * n2
     loop(1, n1, from_first)
     from_core(peer_own)
     loop(1, n1, lambda step: first_pass(first_group(step)))
-
-    def from_second(step, first):
-        group = second_group(step, first)
-        loop(0, depth, lambda k: block_copy(group * depth + k, core_peer).wait_recv())
-        group_copy(group).start()
-
-    loop(1, n2, lambda step: loop(0, n1, lambda first: from_second(step, first)))
-    loop(1, n2, lambda step: from_core(other_half + i1 * n2 + (i2 + step) % n2))
-    loop(1, n2, lambda step: loop(0, n1, lambda first: first_pass(second_group(step, first))))
-    loop(
-        1,
-        n1,
-        lambda step: loop(
-            0, n2, lambda second: from_core(other_half + ((i1 + step) % n1) * n2 + second)
-        ),
-    )
+    if rows_n == width:
+        for place in range(own_last):
+            from_second(place)
+            if place == 0:
+                loop(1, n2, lambda step: from_core(peer_first(step)))
+            else:
+                from_core(peer_second(place - 1))
+            first_pass(second_group(place))
+        from_core(peer_second(own_last - 1))
+    else:
+        loop(0, own_last, from_second)
+        loop(1, n2, lambda step: from_core(peer_first(step)))
+        loop(0, own_last, lambda place: first_pass(second_group(place)))
+        loop(0, peer_last, lambda place: from_core(peer_second(place)))
 
     factor = NACT / (rows * count)
     own_feat = [
@@ -313,15 +330,14 @@
         return factor * out
 
     right_side = select()
-    sides[me] = right_side
+    near[z] = right_side
     total[...] = jnp.zeros_like(total)
 
-    def side_copy(index, peer):
-        return remote(sides.at[index], side_send, side_recv.at[index], peer)
-
-    def side_group(group, peer):
-        rows_of = sides.at[pl.ds(group * depth, depth)]
-        return remote(rows_of, side_send, side_recv_plane.at[group], peer)
+    def near_copy(place, peer):
+        return remote(near.at[place], near_send, near_recv.at[place], peer)
+
+    def side_copy(group, peer):
+        return remote(sides.at[group], side_send, side_recv.at[group], peer)
 
     def show(group):
         meta_all = meta_of(group)
@@ -329,23 +345,23 @@
         logged_feat[group] = rounded(features(jnp.broadcast_to(shown, (NPOL, wide))))
 
     def second_pass(group):
-        base = group * depth
-        low = jnp.concatenate([sides[base + k] for k in range(depth)], axis=1)
-        low = low.astype(BF16).astype(F32)
+        packed = sides[group].astype(F32)
+        low = jnp.concatenate([packed[k * NPOL : (k + 1) * NPOL] for k in range(depth)], axis=1)
         feat = logged_feat[group].astype(F32)
         matched = (feat * jnp.concatenate([low] * NACT, axis=0)).astype(BF16)
         total[...] += nt_dot(matched, grams[group])
 
-    loop(1, depth, lambda step: side_copy(me, z_peer(step)).start())
+    loop(1, depth, lambda step: near_copy(z, z_peer(step)).start())
     loop(0, half_groups, show)
-    loop(1, depth, lambda k: side_copy(own_group * depth + (z + k) % depth, core_peer).wait_recv())
-    loop(1, plane, lambda step: side_group(own_group, plane_peer(step)).start())
+    loop(1, depth, lambda step: near_copy(lax.rem(z + step, depth), core_peer).wait_recv())
+    sides[own_group] = rounded([near[k] for k in range(depth)])
+    loop(1, plane, lambda step: side_copy(own_group, plane_peer(step)).start())
     loop(half_groups, plane, show)
     second_pass(own_group)
 
     def from_plane(step):
-        group = (own_group + step) % plane
-        side_group(group, core_peer).wait_recv()
+        group = lax.rem(own_group + step, plane)
+        side_copy(group, core_peer).wait_recv()
         second_pass(group)
 
     loop(1, plane, from_plane)
@@ -373,7 +389,7 @@
         )
 
         def arrive(step):
-            place = (at + step) % size
+            place = lax.rem(at + step, size)
             remote(slots.at[place], sum_send, recv.at[place], core_peer).wait_recv()
 
         loop(1, size, arrive)
@@ -396,7 +412,8 @@
     remote(
         blocks.at[pl.ds(0, count - 1)], block_send, block_recv.at[0], core_peer
     ).wait_send()
-    remote(sides.at[pl.ds(0, count - 1)], side_send, side_recv.at[0], core_peer).wait_send()
+    remote(near.at[pl.ds(0, depth - 1)], near_send, near_recv.at[0], core_peer).wait_send()
+    remote(sides.at[pl.ds(0, plane - 1)], side_send, side_recv.at[0], core_peer).wait_send()
     remote(
         near_sums.at[pl.ds(0, depth - 1)], sum_send, sum_recv.at[0], core_peer
     ).wait_send()
@@ -419,7 +436,8 @@
         out_specs=vmem,
         scratch_shapes=[
             pltpu.VMEM((count, rows + META, dims), BF16),
-            pltpu.VMEM((count, NPOL, rows), F32),
+            pltpu.VMEM((depth, NPOL, rows), F32),
+            pltpu.VMEM((plane, depth * NPOL, rows), BF16),
             pltpu.VMEM((plane, rows, depth * rows), BF16),
             pltpu.VMEM((plane, NPOL * NACT, depth * rows), BF16),
             pltpu.VMEM((NPOL * NACT, rows), F32),
@@ -432,14 +450,15 @@
             pltpu.SemaphoreType.DMA,
             pltpu.SemaphoreType.DMA((count,)),
             pltpu.SemaphoreType.DMA,
-            pltpu.SemaphoreType.DMA((count,)),
+            pltpu.SemaphoreType.DMA((depth,)),
+            pltpu.SemaphoreType.DMA,
             pltpu.SemaphoreType.DMA((plane,)),
             pltpu.SemaphoreType.DMA,
             pltpu.SemaphoreType.DMA((depth,)),
             pltpu.SemaphoreType.DMA((plane,)),
         ],
         compiler_params=pltpu.CompilerParams(
-            collective_id=0, has_side_effects=True, vmem_limit_bytes=60 * 1024 * 1024
+            collective_id=0, has_side_effects=True, vmem_limit_bytes=48 * 1024 * 1024
         ),
     )(contexts, logged_actions.reshape(1, rows), policy_actions.T, rewards.reshape(1, rows))
     return results[0:NPOL].T, results[NPOL : 2 * NPOL].T, results[2 * NPOL, 0:NPOL]

time: 40.1 us -> 37.4 us (0.933)
  Pallas kernels: 36.7 us -> 34 us
    pallas_call x1, Pallas kernels: 36.7 us -> 34 us  [on_device(): pl.pallas_call(functools.partial(kernel, sizes), out_shape=jax.ShapeDtype...]
    unnamed x0 -> x8, local copies, waits for them, and re-layouts: none -> 1.43 us
    squeeze x1, local copies, waits for them, and re-layouts: 1.19 us -> 0.51 us  [on_device(): results[2 * NPOL, 0:NPOL]]
    transpose x1, local copies, waits for them, and re-layouts: 1.28 us -> 0.6 us  [on_device(): results[NPOL:2 * NPOL]]
where the time goes in v3:
time: 37.4 us; the launch traced here: 37.2 us
  Pallas kernels  34 us (91%)
  local copies, waits for them, and re-layouts  2.54 us (7%)
  between operations  0.67 us (2%)
    pallas_call x1, Pallas kernels, on_device(): pl.pallas_call(functools.partial(kernel, sizes), out_shape=jax.ShapeDtype...  34 us
    unnamed x8, local copies, waits for them, and re-layouts  1.43 us

profile of v3, /device:TPU:0, one launch (start us, length us, event | category | flops | bytes accessed | tf_op | source)
XLA Modules:
  0.0 37.2 jit_solution(4511678017930691716)
XLA Ops:
  0.6 0.0 copy-start.1
  0.6 0.0 copy-start.2
  0.7 0.0 copy-start.3
  0.7 0.7 %copy-done.1 = s32[128,8]{0,1:T(8,128)S(1)} copy-done((s32[128,8]{0,1:T(8,128)S(1)}, s32[128,8]{0,1:T(8,128)}, u32[]{:S(2)}) %copy-start.1) | copy-done | bytes 4120
  1.3 0.0 copy-done.2
  1.3 0.0 copy-done.3
  1.3 0.0 copy-start
  1.3 0.8 %copy-done = bf16[128,128]{1,0:T(8,128)(2,1)S(1)} copy-done((bf16[128,128]{1,0:T(8,128)(2,1)S(1)}, bf16[128,128]{1,0:T(8,128)(2,1)}, u32[]{:S(2)}) %copy-start) | copy-done | bytes 32792
  2.1 34.0 %shard_map.67 = f32[24,128]{1,0:T(8,128)S(1)} custom-call(bf16[128,128]{1,0:T(8,128)(2,1)S(1)} %copy-done, s32[1,128]{1,0:T(1,128)S(1)} %bitcast.10, s32[8,128]{1,0:T(8,128)S(1)} %bitcast.9, f32[1,128]{1,0:T(1,128)S(1)} %bitcast.11), custom_call_target="tpu_custom_call" | custom-call | tf_op jit(solution)/shard_map/pallas_call | solution.py:432
  36.1 0.6 %slice_bitcast_fusion = (f32[128,8]{0,1:T(8,128)}, f32[128,8]{0,1:T(8,128)}) fusion(f32[24,128]{1,0:T(8,128)S(1)} %shard_map.67), kind=kLoop, calls=%fused_computation | loop fusion | bytes 16384 | tf_op jit(solution)/shard_map/transpose | solution.py:464
  36.7 0.5 %slice_bitcast_fusion.2 = f32[8]{0:T(128)} fusion(f32[24,128]{1,0:T(8,128)S(1)} %shard_map.67), kind=kLoop, calls=%fused_computation.2 | loop fusion | bytes 64 | tf_op jit(solution)/shard_map/squeeze | solution.py:464
Async XLA Ops:
  0.6 0.7 %copy-start.1 = (s32[128,8]{0,1:T(8,128)S(1)}, s32[128,8]{0,1:T(8,128)}, u32[]{:S(2)}) copy-start(s32[128,8]{0,1:T(8,128)} %param.6) | copy-start | bytes 12292
  0.6 0.7 %copy-start.2 = (s32[128]{0:T(128)S(1)}, s32[128]{0:T(128)}, u32[]{:S(2)}) copy-start(s32[128]{0:T(128)} %param.5) | copy-start | bytes 1540
  0.7 0.7 %copy-start.3 = (f32[128]{0:T(128)S(1)}, f32[128]{0:T(128)}, u32[]{:S(2)}) copy-start(f32[128]{0:T(128)} %param.7) | copy-start | bytes 1540
  1.3 0.8 %copy-start = (bf16[128,128]{1,0:T(8,128)(2,1)S(1)}, bf16[128,128]{1,0:T(8,128)(2,1)}, u32[]{:S(2)}) copy-start(bf16[128,128]{1,0:T(8,128)(2,1)} %ctx_ref.1) | copy-start | bytes 98308

commit v4 on v3

--- a/solution.py
+++ b/solution.py
@@ -64,8 +64,8 @@
     return jnp.concatenate(parts, axis=0).astype(BF16)
 
 
-def nt_dot(left, right):
-    return lax.dot_general(left, right, (((1,), (1,)), ((), ())), preferred_element_type=F32)
+def dot(left, right, over=1):
+    return lax.dot_general(left, right, (((over,), (0,)), ((), ())), preferred_element_type=F32)
 
 
 def kernel(
@@ -81,12 +81,8 @@
     grams,
     logged_feat,
     total,
-    logged_own,
-    policy_own,
-    reward_own,
     near_sums,
     plane_sums,
-    load_sem,
     block_send,
     block_recv,
     near_send,
@@ -151,35 +147,23 @@
     loop(1, depth, lambda step: greet(z_peer(step)))
     loop(1, plane, lambda step: greet(plane_peer(step)))
 
-    loads = [
-        pltpu.make_async_copy(source, target, load_sem.at[place])
-        for place, (source, target) in enumerate(
-            (
-                (ctx_ref, blocks.at[me, pl.ds(0, rows)]),
-                (logged_ref, logged_own),
-                (policy_ref, policy_own),
-                (reward_ref, reward_own),
-            )
-        )
-    ]
-    for load in loads:
-        load.start()
-    for load in loads:
-        load.wait()
-
-    own = blocks[me, 0:rows, :]
+    own = ctx_ref[...]
+    blocks[me, 0:rows, :] = own
     own_wide = own.astype(F32)
     own_squares = jnp.sum(own_wide * own_wide, axis=1, keepdims=True) * (1.0 / dims)
     here = lax.broadcasted_iota(jnp.int32, (rows, rows), 0)
     there = lax.broadcasted_iota(jnp.int32, (rows, rows), 1)
     squares_row = jnp.sum(jnp.where(here == there, own_squares, 0.0), axis=0, keepdims=True)
+    own_turned = own_wide.T.astype(BF16)
+    place = lax.broadcasted_iota(jnp.int32, (META // 2, rows), 0)
+    picks = jnp.where((place >= 9) & (place <= 11), -0.5 * dims, 0.0).astype(BF16)
 
     def pieces(value):
         high = jnp.floor(value * (1.0 / 512.0) + 0.5)
         return high, value - 512.0 * high
 
-    policy_high, policy_low = pieces(policy_own[...].astype(F32))
-    logged_high, logged_low = pieces(logged_own[...].astype(F32))
+    policy_high, policy_low = pieces(policy_ref[...].astype(F32))
+    logged_high, logged_low = pieces(logged_ref[...].astype(F32))
     square_1 = squares_row.astype(BF16).astype(F32)
     square_2 = (squares_row - square_1).astype(BF16).astype(F32)
     square_3 = squares_row - square_1 - square_2
@@ -235,13 +219,15 @@
         base = group * depth
         meta_all = meta_of(group)
         policy = (meta_all[0:8] * 512.0 + meta_all[8:16]).astype(jnp.int32)
-        squares = meta_all[25:26] + meta_all[26:27] + meta_all[27:28]
         others = jnp.concatenate([blocks[base + k, 0:rows, :] for k in range(depth)], axis=0)
-        inner = nt_dot(own, others)
+        squares = jnp.concatenate(
+            [blocks[base + k, rows + META // 2 : rows + META, :] for k in range(depth)], axis=1
+        )
+        inner = dot(others, own_turned) + dot(squares, picks, 0)
         policy_feat = rounded(features(policy))
-        gram = jnp.exp(inner * (2.0 / dims) - own_squares - squares).astype(BF16)
+        gram = jnp.exp(inner * (2.0 / dims) - squares_row).astype(BF16)
         grams[group] = gram
-        total[...] += nt_dot(policy_feat, gram)
+        total[...] += dot(policy_feat, gram)
 
     def from_core(group):
         group_copy(group).wait_recv()
@@ -319,7 +305,7 @@
     factor = NACT / (rows * count)
     own_feat = [
         part.astype(BF16).astype(F32)
-        for part in features(jnp.broadcast_to(logged_own[...], (NPOL, rows)))
+        for part in features(jnp.broadcast_to(logged_ref[...], (NPOL, rows)))
     ]
 
     def select():
@@ -349,7 +335,7 @@
         low = jnp.concatenate([packed[k * NPOL : (k + 1) * NPOL] for k in range(depth)], axis=1)
         feat = logged_feat[group].astype(F32)
         matched = (feat * jnp.concatenate([low] * NACT, axis=0)).astype(BF16)
-        total[...] += nt_dot(matched, grams[group])
+        total[...] += dot(matched, grams[group])
 
     loop(1, depth, lambda step: near_copy(z, z_peer(step)).start())
     loop(0, half_groups, show)
@@ -377,7 +363,7 @@
     partial = (
         to_row(right_side * right_side, 0)
         + to_row(right_side * image, NPOL)
-        + to_row(reward_own[...] * right_side, 2 * NPOL)
+        + to_row(reward_ref[...] * right_side, 2 * NPOL)
     )
 
     def all_sum(value, slots, recv, at, size, peer_of):
@@ -428,25 +414,20 @@
     plane = 2 * rows_n * width
     count = plane * depth
     vmem = pl.BlockSpec(memory_space=pltpu.VMEM)
-    hbm = pl.BlockSpec(memory_space=pltpu.HBM)
     results = pl.pallas_call(
         functools.partial(kernel, sizes),
         out_shape=jax.ShapeDtypeStruct((3 * NPOL, rows), F32),
-        in_specs=[hbm] * 4,
+        in_specs=[vmem] * 4,
         out_specs=vmem,
         scratch_shapes=[
             pltpu.VMEM((count, rows + META, dims), BF16),
             pltpu.VMEM((depth, NPOL, rows), F32),
             pltpu.VMEM((plane, depth * NPOL, rows), BF16),
-            pltpu.VMEM((plane, rows, depth * rows), BF16),
+            pltpu.VMEM((plane, depth * rows, rows), BF16),
             pltpu.VMEM((plane, NPOL * NACT, depth * rows), BF16),
             pltpu.VMEM((NPOL * NACT, rows), F32),
-            pltpu.VMEM((1, rows), jnp.int32),
-            pltpu.VMEM((NPOL, rows), jnp.int32),
-            pltpu.VMEM((1, rows), F32),
             pltpu.VMEM((depth, 1, rows), F32),
             pltpu.VMEM((plane, 1, rows), F32),
-            pltpu.SemaphoreType.DMA((4,)),
             pltpu.SemaphoreType.DMA,
             pltpu.SemaphoreType.DMA((count,)),
             pltpu.SemaphoreType.DMA,

time: 37.4 us -> 37.5 us (level)
  no operation moved by 1% of the time
where the time goes in v4:
time: 37.5 us; the launch traced here: 37.3 us
  Pallas kernels  34.1 us (91%)
  local copies, waits for them, and re-layouts  2.54 us (7%)
  between operations  0.67 us (2%)
    pallas_call x1, Pallas kernels, on_device(): pl.pallas_call(functools.partial(kernel, sizes), out_shape=jax.ShapeDtype...  34.1 us
    unnamed x8, local copies, waits for them, and re-layouts  1.43 us

profile of v4, /device:TPU:0, one launch (start us, length us, event | category | flops | bytes accessed | tf_op | source)
XLA Modules:
  0.0 37.3 jit_solution(4447475022513357716)
XLA Ops:
  0.6 0.0 copy-start.1
  0.6 0.0 copy-start.2
  0.7 0.0 copy-start.3
  0.7 0.7 %copy-done.1 = s32[128,8]{0,1:T(8,128)S(1)} copy-done((s32[128,8]{0,1:T(8,128)S(1)}, s32[128,8]{0,1:T(8,128)}, u32[]{:S(2)}) %copy-start.1) | copy-done | bytes 4120
  1.3 0.0 copy-done.2
  1.3 0.0 copy-done.3
  1.3 0.0 copy-start
  1.3 0.8 %copy-done = bf16[128,128]{1,0:T(8,128)(2,1)S(1)} copy-done((bf16[128,128]{1,0:T(8,128)(2,1)S(1)}, bf16[128,128]{1,0:T(8,128)(2,1)}, u32[]{:S(2)}) %copy-start) | copy-done | bytes 32792
  2.1 34.1 %shard_map.67 = f32[24,128]{1,0:T(8,128)S(1)} custom-call(bf16[128,128]{1,0:T(8,128)(2,1)S(1)} %copy-done, s32[1,128]{1,0:T(1,128)S(1)} %bitcast.10, s32[8,128]{1,0:T(8,128)S(1)} %bitcast.9, f32[1,128]{1,0:T(1,128)S(1)} %bitcast.11), custom_call_target="tpu_custom_call" | custom-call | tf_op jit(solution)/shard_map/pallas_call | solution.py:417
  36.2 0.6 %slice_bitcast_fusion = (f32[128,8]{0,1:T(8,128)}, f32[128,8]{0,1:T(8,128)}) fusion(f32[24,128]{1,0:T(8,128)S(1)} %shard_map.67), kind=kLoop, calls=%fused_computation | loop fusion | bytes 16384 | tf_op jit(solution)/shard_map/transpose | solution.py:445
  36.8 0.5 %slice_bitcast_fusion.2 = f32[8]{0:T(128)} fusion(f32[24,128]{1,0:T(8,128)S(1)} %shard_map.67), kind=kLoop, calls=%fused_computation.2 | loop fusion | bytes 64 | tf_op jit(solution)/shard_map/squeeze | solution.py:445
Async XLA Ops:
  0.6 0.7 %copy-start.1 = (s32[128,8]{0,1:T(8,128)S(1)}, s32[128,8]{0,1:T(8,128)}, u32[]{:S(2)}) copy-start(s32[128,8]{0,1:T(8,128)} %param.6) | copy-start | bytes 12292
  0.6 0.7 %copy-start.2 = (s32[128]{0:T(128)S(1)}, s32[128]{0:T(128)}, u32[]{:S(2)}) copy-start(s32[128]{0:T(128)} %param.5) | copy-start | bytes 1540
  0.7 0.7 %copy-start.3 = (f32[128]{0:T(128)S(1)}, f32[128]{0:T(128)}, u32[]{:S(2)}) copy-start(f32[128]{0:T(128)} %param.7) | copy-start | bytes 1540
  1.3 0.8 %copy-start = (bf16[128,128]{1,0:T(8,128)(2,1)S(1)}, bf16[128,128]{1,0:T(8,128)(2,1)}, u32[]{:S(2)}) copy-start(bf16[128,128]{1,0:T(8,128)(2,1)} %ctx_ref.1) | copy-start | bytes 98308

commit v5 on v4

--- a/solution.py
+++ b/solution.py
@@ -76,6 +76,11 @@
     reward_ref,
     results_ref,
     blocks,
+    mate,
+    part_out,
+    part_in,
+    image_out,
+    image_in,
     near,
     sides,
     grams,
@@ -85,6 +90,8 @@
     plane_sums,
     block_send,
     block_recv,
+    pair_send,
+    pair_recv,
     near_send,
     near_recv,
     side_send,
@@ -112,8 +119,8 @@
     n2 = inner_size(1 - core)
     i1 = y + core * (x - y)
     i2 = x + core * (y - x)
-    own_half = core * half_groups
-    own_group = own_half + i2 * n1 + i1
+    own_group = i2 * n1 + i1
+    own_plane = core * half_groups + own_group
     me = own_group * depth + z
 
     def device(first, second, at_z, at_core):
@@ -131,11 +138,15 @@
         return device(i1, lax.rem(i2 + step, n2), z, core)
 
     def plane_peer(step):
-        group = lax.rem(own_group + step, plane)
+        group = lax.rem(own_plane + step, plane)
         at_core = lax.div(group, half_groups)
         place = lax.rem(group, half_groups)
         inside = inner_size(at_core)
         return device(lax.rem(place, inside), lax.div(place, inside), z, at_core)
+
+    def half_peer(step):
+        place = lax.rem(own_group + step, half_groups)
+        return device(lax.rem(place, n1), lax.div(place, n1), z, core)
 
     core_peer = (x, (z * width + y) * 2 + 1 - core)
 
@@ -154,9 +165,9 @@
     here = lax.broadcasted_iota(jnp.int32, (rows, rows), 0)
     there = lax.broadcasted_iota(jnp.int32, (rows, rows), 1)
     squares_row = jnp.sum(jnp.where(here == there, own_squares, 0.0), axis=0, keepdims=True)
-    own_turned = own_wide.T.astype(BF16)
     place = lax.broadcasted_iota(jnp.int32, (META // 2, rows), 0)
     picks = jnp.where((place >= 9) & (place <= 11), -0.5 * dims, 0.0).astype(BF16)
+    picks = jnp.concatenate([picks, picks], axis=1)
 
     def pieces(value):
         high = jnp.floor(value * (1.0 / 512.0) + 0.5)
@@ -197,10 +208,6 @@
     def block_copy(index, peer):
         return remote(blocks.at[index], block_send, block_recv.at[index], peer)
 
-    def group_copy(group):
-        start = group * depth
-        return remote(blocks.at[pl.ds(start, depth)], block_send, block_recv.at[start], core_peer)
-
     def to_first(index):
         loop(1, n1, lambda step: block_copy(index, first_peer(step)).start())
 
@@ -223,19 +230,33 @@
         squares = jnp.concatenate(
             [blocks[base + k, rows + META // 2 : rows + META, :] for k in range(depth)], axis=1
         )
-        inner = dot(others, own_turned) + dot(squares, picks, 0)
+        inner = dot(others, pair_turned) + dot(squares, picks, 0)
         policy_feat = rounded(features(policy))
-        gram = jnp.exp(inner * (2.0 / dims) - squares_row).astype(BF16)
+        gram = jnp.exp(inner * (2.0 / dims) - pair_squares).astype(BF16)
         grams[group] = gram
         total[...] += dot(policy_feat, gram)
 
-    def from_core(group):
-        group_copy(group).wait_recv()
-        first_pass(group)
-
+    mate_copy = pltpu.make_async_remote_copy(
+        src_ref=blocks.at[me],
+        dst_ref=mate,
+        send_sem=block_send,
+        recv_sem=pair_recv.at[0],
+        device_id=core_peer,
+        device_id_type=MESH,
+    )
     loop(1, depth, lambda step: block_copy(me, z_peer(step)).start())
     to_first(me)
     to_second(me)
+    mate_copy.start()
+
+    mate_copy.wait_recv()
+    mate_wide = mate[0:rows, :].astype(F32)
+    mate_meta = mate[rows : rows + META, :].astype(F32)
+    mate_squares = mate_meta[25:26] + mate_meta[26:27] + mate_meta[27:28]
+    mate_logged = (mate_meta[16:17] * 512.0 + mate_meta[24:25]).astype(jnp.int32)
+    pair_turned = jnp.concatenate([own_wide.T, mate_wide.T], axis=1).astype(BF16)
+    pair_squares = jnp.concatenate([squares_row, mate_squares], axis=1)
+    pair_logged = jnp.concatenate([logged_ref[...], mate_logged], axis=1)
 
     def from_z(step):
         index = own_group * depth + lax.rem(z + step, depth)
@@ -244,19 +265,10 @@
         to_second(index)
 
     loop(1, depth, from_z)
-    group_copy(own_group).start()
     first_pass(own_group)
 
     def first_group(step):
-        return own_half + i2 * n1 + lax.rem(i1 + step, n1)
-
-    def second_group(place):
-        step = 1 + lax.div(place, n1)
-        first = lax.rem(i1 + lax.rem(place, n1), n1)
-        return own_half + lax.rem(i2 + step, n2) * n1 + first
-
-    other_half = half_groups - own_half
-    peer_own = other_half + i1 * n2 + i2
+        return i2 * n1 + lax.rem(i1 + step, n1)
 
     def from_first(step):
         group = first_group(step)
@@ -267,45 +279,23 @@
             to_second(index)
 
         loop(0, depth, one)
-        group_copy(group).start()
-
-    def peer_first(step):
-        return other_half + i1 * n2 + lax.rem(i2 + step, n2)
-
-    def peer_second(place):
-        step = 1 + lax.div(place, n2)
-        second = lax.rem(i2 + lax.rem(place, n2), n2)
-        return other_half + lax.rem(i1 + step, n1) * n2 + second
+
+    loop(1, n1, from_first)
+    loop(1, n1, lambda step: first_pass(first_group(step)))
 
     def from_second(place):
-        group = second_group(place)
+        step = 1 + lax.div(place, n1)
+        first = lax.rem(i1 + lax.rem(place, n1), n1)
+        group = lax.rem(i2 + step, n2) * n1 + first
         loop(0, depth, lambda k: block_copy(group * depth + k, core_peer).wait_recv())
-        group_copy(group).start()
-
-    own_last = (n2 - 1) * n1
-    peer_last = (n1 - 1) * n2
-    loop(1, n1, from_first)
-    from_core(peer_own)
-    loop(1, n1, lambda step: first_pass(first_group(step)))
-    if rows_n == width:
-        for place in range(own_last):
-            from_second(place)
-            if place == 0:
-                loop(1, n2, lambda step: from_core(peer_first(step)))
-            else:
-                from_core(peer_second(place - 1))
-            first_pass(second_group(place))
-        from_core(peer_second(own_last - 1))
-    else:
-        loop(0, own_last, from_second)
-        loop(1, n2, lambda step: from_core(peer_first(step)))
-        loop(0, own_last, lambda place: first_pass(second_group(place)))
-        loop(0, peer_last, lambda place: from_core(peer_second(place)))
+        first_pass(group)
+
+    loop(0, (n2 - 1) * n1, from_second)
 
     factor = NACT / (rows * count)
     own_feat = [
         part.astype(BF16).astype(F32)
-        for part in features(jnp.broadcast_to(logged_ref[...], (NPOL, rows)))
+        for part in features(jnp.broadcast_to(pair_logged, (NPOL, 2 * rows)))
     ]
 
     def select():
@@ -315,20 +305,42 @@
             out += own_feat[level] * value[level * NPOL : (level + 1) * NPOL]
         return factor * out
 
-    right_side = select()
-    near[z] = right_side
-    total[...] = jnp.zeros_like(total)
-
-    def near_copy(place, peer):
-        return remote(near.at[place], near_send, near_recv.at[place], peer)
-
-    def side_copy(group, peer):
-        return remote(sides.at[group], side_send, side_recv.at[group], peer)
-
     def show(group):
         meta_all = meta_of(group)
         shown = (meta_all[16:17] * 512.0 + meta_all[24:25]).astype(jnp.int32)
         logged_feat[group] = rounded(features(jnp.broadcast_to(shown, (NPOL, wide))))
+
+    def pair_copy(source, target, at):
+        return pltpu.make_async_remote_copy(
+            src_ref=source,
+            dst_ref=target,
+            send_sem=pair_send.at[at],
+            recv_sem=pair_recv.at[1 + at],
+            device_id=core_peer,
+            device_id_type=MESH,
+        )
+
+    def add_pair(mine, other):
+        return (
+            mine[:, 0:rows] + other[:, rows : 2 * rows],
+            mine[:, rows : 2 * rows] + other[:, 0:rows],
+        )
+
+    part = select()
+    part_out[...] = part
+    part_copy = pair_copy(part_out, part_in, 0)
+    part_copy.start()
+    loop(0, half_groups // 2, show)
+    part_copy.wait_recv()
+    right_side, mate_side = add_pair(part, part_in[...])
+    near[z] = right_side
+    total[...] = jnp.zeros_like(total)
+
+    def near_copy(place, peer):
+        return remote(near.at[place], near_send, near_recv.at[place], peer)
+
+    def side_copy(group, peer):
+        return remote(sides.at[group], side_send, side_recv.at[group], peer)
 
     def second_pass(group):
         packed = sides[group].astype(F32)
@@ -338,20 +350,24 @@
         total[...] += dot(matched, grams[group])
 
     loop(1, depth, lambda step: near_copy(z, z_peer(step)).start())
-    loop(0, half_groups, show)
+    loop(half_groups // 2, half_groups, show)
     loop(1, depth, lambda step: near_copy(lax.rem(z + step, depth), core_peer).wait_recv())
     sides[own_group] = rounded([near[k] for k in range(depth)])
-    loop(1, plane, lambda step: side_copy(own_group, plane_peer(step)).start())
-    loop(half_groups, plane, show)
+    loop(1, half_groups, lambda step: side_copy(own_group, half_peer(step)).start())
     second_pass(own_group)
 
     def from_plane(step):
-        group = lax.rem(own_group + step, plane)
+        group = lax.rem(own_group + step, half_groups)
         side_copy(group, core_peer).wait_recv()
         second_pass(group)
 
-    loop(1, plane, from_plane)
-    image = select() + RIDGE * right_side
+    loop(1, half_groups, from_plane)
+    image_part = select()
+    image_out[...] = image_part
+    image_copy = pair_copy(image_out, image_in, 1)
+    image_copy.start()
+    own_square = right_side * right_side
+    curved = image_part[:, 0:rows] * right_side + image_part[:, rows : 2 * rows] * mate_side
 
     lane = lax.broadcasted_iota(jnp.int32, (NPOL, rows), 1)
     sub = lax.broadcasted_iota(jnp.int32, (NPOL, rows), 0)
@@ -361,8 +377,8 @@
         return jnp.sum(jnp.where(lane == sub + offset, column, 0.0), axis=0, keepdims=True)
 
     partial = (
-        to_row(right_side * right_side, 0)
-        + to_row(right_side * image, NPOL)
+        to_row(own_square, 0)
+        + to_row(curved + RIDGE * own_square, NPOL)
         + to_row(reward_ref[...] * right_side, 2 * NPOL)
     )
 
@@ -382,7 +398,9 @@
         return jnp.sum(slots[...], axis=0)
 
     partial = all_sum(partial, near_sums, sum_recv, z, depth, z_peer)
-    partial = all_sum(partial, plane_sums, sum_recv_plane, own_group, plane, plane_peer)
+    partial = all_sum(partial, plane_sums, sum_recv_plane, own_plane, plane, plane_peer)
+    image_copy.wait_recv()
+    image = add_pair(image_part, image_in[...])[0] + RIDGE * right_side
 
     def to_column(offset):
         spread_row = jnp.broadcast_to(partial, (NPOL, rows))
@@ -396,10 +414,12 @@
     results_ref[2 * NPOL :] = jnp.broadcast_to(values_row, (NPOL, rows))
 
     remote(
-        blocks.at[pl.ds(0, count - 1)], block_send, block_recv.at[0], core_peer
+        blocks, block_send, block_recv.at[0], core_peer
     ).wait_send()
+    part_copy.wait_send()
+    image_copy.wait_send()
     remote(near.at[pl.ds(0, depth - 1)], near_send, near_recv.at[0], core_peer).wait_send()
-    remote(sides.at[pl.ds(0, plane - 1)], side_send, side_recv.at[0], core_peer).wait_send()
+    remote(sides.at[pl.ds(0, half_groups - 1)], side_send, side_recv.at[0], core_peer).wait_send()
     remote(
         near_sums.at[pl.ds(0, depth - 1)], sum_send, sum_recv.at[0], core_peer
     ).wait_send()
@@ -411,8 +431,8 @@
 def on_device(sizes, contexts, logged_actions, policy_actions, rewards):
     rows_n, depth, width = sizes
     rows, dims = contexts.shape
-    plane = 2 * rows_n * width
-    count = plane * depth
+    half_groups = rows_n * width
+    plane = 2 * half_groups
     vmem = pl.BlockSpec(memory_space=pltpu.VMEM)
     results = pl.pallas_call(
         functools.partial(kernel, sizes),
@@ -420,20 +440,27 @@
         in_specs=[vmem] * 4,
         out_specs=vmem,
         scratch_shapes=[
-            pltpu.VMEM((count, rows + META, dims), BF16),
+            pltpu.VMEM((half_groups * depth, rows + META, dims), BF16),
+            pltpu.VMEM((rows + META, dims), BF16),
+            pltpu.VMEM((NPOL, 2 * rows), F32),
+            pltpu.VMEM((NPOL, 2 * rows), F32),
+            pltpu.VMEM((NPOL, 2 * rows), F32),
+            pltpu.VMEM((NPOL, 2 * rows), F32),
             pltpu.VMEM((depth, NPOL, rows), F32),
-            pltpu.VMEM((plane, depth * NPOL, rows), BF16),
-            pltpu.VMEM((plane, depth * rows, rows), BF16),
-            pltpu.VMEM((plane, NPOL * NACT, depth * rows), BF16),
-            pltpu.VMEM((NPOL * NACT, rows), F32),
+            pltpu.VMEM((half_groups, depth * NPOL, rows), BF16),
+            pltpu.VMEM((half_groups, depth * rows, 2 * rows), BF16),
+            pltpu.VMEM((half_groups, NPOL * NACT, depth * rows), BF16),
+            pltpu.VMEM((NPOL * NACT, 2 * rows), F32),
             pltpu.VMEM((depth, 1, rows), F32),
             pltpu.VMEM((plane, 1, rows), F32),
             pltpu.SemaphoreType.DMA,
-            pltpu.SemaphoreType.DMA((count,)),
+            pltpu.SemaphoreType.DMA((half_groups * depth,)),
+            pltpu.SemaphoreType.DMA((2,)),
+            pltpu.SemaphoreType.DMA((3,)),
             pltpu.SemaphoreType.DMA,
             pltpu.SemaphoreType.DMA((depth,)),
             pltpu.SemaphoreType.DMA,
-            pltpu.SemaphoreType.DMA((plane,)),
+            pltpu.SemaphoreType.DMA((half_groups,)),
             pltpu.SemaphoreType.DMA,
             pltpu.SemaphoreType.DMA((depth,)),
             pltpu.SemaphoreType.DMA((plane,)),

time: 37.5 us -> 36.7 us (0.979)
  Pallas kernels: 34.1 us -> 33.2 us
    pallas_call x1, Pallas kernels: 34.1 us -> 33.2 us  [on_device(): pl.pallas_call(functools.partial(kernel, sizes), out_shape=jax.ShapeDtype...]
where the time goes in v5:
time: 36.7 us; the launch traced here: 36.4 us
  Pallas kernels  33.2 us (90%)
  local copies, waits for them, and re-layouts  2.54 us (7%)
  between operations  0.67 us (2%)
    pallas_call x1, Pallas kernels, on_device(): pl.pallas_call(functools.partial(kernel, sizes), out_shape=jax.ShapeDtype...  33.2 us
    unnamed x8, local copies, waits for them, and re-layouts  1.43 us

profile of v5, /device:TPU:0, one launch (start us, length us, event | category | flops | bytes accessed | tf_op | source)
XLA Modules:
  0.0 36.4 jit_solution(14821045738752499498)
XLA Ops:
  0.6 0.0 copy-start.1
  0.6 0.0 copy-start.2
  0.7 0.0 copy-start.3
  0.7 0.7 %copy-done.1 = s32[128,8]{0,1:T(8,128)S(1)} copy-done((s32[128,8]{0,1:T(8,128)S(1)}, s32[128,8]{0,1:T(8,128)}, u32[]{:S(2)}) %copy-start.1) | copy-done | bytes 4120
  1.3 0.0 copy-done.2
  1.3 0.0 copy-done.3
  1.3 0.0 copy-start
  1.3 0.8 %copy-done = bf16[128,128]{1,0:T(8,128)(2,1)S(1)} copy-done((bf16[128,128]{1,0:T(8,128)(2,1)S(1)}, bf16[128,128]{1,0:T(8,128)(2,1)}, u32[]{:S(2)}) %copy-start) | copy-done | bytes 32792
  2.1 33.2 %shard_map.67 = f32[24,128]{1,0:T(8,128)S(1)} custom-call(bf16[128,128]{1,0:T(8,128)(2,1)S(1)} %copy-done, s32[1,128]{1,0:T(1,128)S(1)} %bitcast.10, s32[8,128]{1,0:T(8,128)S(1)} %bitcast.9, f32[1,128]{1,0:T(1,128)S(1)} %bitcast.11), custom_call_target="tpu_custom_call" | custom-call | tf_op jit(solution)/shard_map/pallas_call | solution.py:437
  35.3 0.6 %slice_bitcast_fusion = (f32[128,8]{0,1:T(8,128)}, f32[128,8]{0,1:T(8,128)}) fusion(f32[24,128]{1,0:T(8,128)S(1)} %shard_map.67), kind=kLoop, calls=%fused_computation | loop fusion | bytes 16384 | tf_op jit(solution)/shard_map/transpose | solution.py:472
  35.9 0.5 %slice_bitcast_fusion.2 = f32[8]{0:T(128)} fusion(f32[24,128]{1,0:T(8,128)S(1)} %shard_map.67), kind=kLoop, calls=%fused_computation.2 | loop fusion | bytes 64 | tf_op jit(solution)/shard_map/squeeze | solution.py:472
Async XLA Ops:
  0.6 0.7 %copy-start.1 = (s32[128,8]{0,1:T(8,128)S(1)}, s32[128,8]{0,1:T(8,128)}, u32[]{:S(2)}) copy-start(s32[128,8]{0,1:T(8,128)} %param.6) | copy-start | bytes 12292
  0.6 0.7 %copy-start.2 = (s32[128]{0:T(128)S(1)}, s32[128]{0:T(128)}, u32[]{:S(2)}) copy-start(s32[128]{0:T(128)} %param.5) | copy-start | bytes 1540
  0.7 0.7 %copy-start.3 = (f32[128]{0:T(128)S(1)}, f32[128]{0:T(128)}, u32[]{:S(2)}) copy-start(f32[128]{0:T(128)} %param.7) | copy-start | bytes 1540
  1.3 0.8 %copy-start = (bf16[128,128]{1,0:T(8,128)(2,1)S(1)}, bf16[128,128]{1,0:T(8,128)(2,1)}, u32[]{:S(2)}) copy-start(bf16[128,128]{1,0:T(8,128)(2,1)} %ctx_ref.1) | copy-start | bytes 98308

commit v6 on v5

v6 whole, which is shorter than its diff:
```python
import functools
import math

import jax
import jax.numpy as jnp
from jax import lax
from jax.experimental import pallas as pl
from jax.experimental.pallas import tpu as pltpu
from jax.sharding import PartitionSpec as P

MESH = pl.DeviceIdType.MESH
F32 = jnp.float32
BF16 = jnp.bfloat16

NPOL = 8
NACT = 16
CATALOG = 131042
RIDGE = 0.1
STRIDE = 1009
PHASE = 0.37
TWO_PI = 2.0 * math.pi
META = 32


def loop(low, high, body):
    if isinstance(low, int) and isinstance(high, int) and high - low <= 4:
        for step in range(low, high):
            body(step)
    else:

        def wrapped(step, carried):
            body(step)
            return carried

        lax.fori_loop(low, high, wrapped, 0)


def cosine(turned, phase):
    whole = jnp.floor(turned.astype(F32) * (1.0 / CATALOG) + 0.5).astype(jnp.int32)
    rest = (turned - whole * CATALOG).astype(F32)
    turns = rest * (1.0 / CATALOG) + phase / TWO_PI
    turns = turns - jnp.floor(turns + 0.5)
    angle = TWO_PI * (0.25 - jnp.abs(turns))
    square = angle * angle
    series = -1.0 / 39916800.0
    for term in (362880.0, -5040.0, 120.0, -6.0, 1.0):
        series = series * square + 1.0 / term
    return series * angle


def features(chosen):
    twice = 2.0 * cosine(chosen * STRIDE, PHASE)
    before = cosine(chosen, 0.0)
    now = cosine(chosen * (1 + STRIDE), PHASE)
    scale = math.sqrt(2.0 / NACT)
    out = [jnp.full(chosen.shape, 1.0 / math.sqrt(NACT), F32)]
    for level in range(1, NACT):
        out.append(scale * now)
        before, now = now, twice * now - before
    return out


def rounded(parts):
    return jnp.concatenate(parts, axis=0).astype(BF16)


def dot(left, right, over=1):
    return lax.dot_general(left, right, (((over,), (0,)), ((), ())), preferred_element_type=F32)


def kernel(
    sizes,
    ctx_ref,
    logged_ref,
    policy_ref,
    reward_ref,
    results_ref,
    blocks,
    team,
    parts,
    team_sides,
    image_out,
    image_in,
    near,
    sides,
    grams,
    logged_feat,
    total,
    near_sums,
    plane_sums,
    block_send,
    block_recv,
    team_send,
    team_recv,
    part_send,
    part_recv,
    image_send,
    image_recv,
    near_send,
    near_recv,
    side_send,
    side_recv,
    sum_send,
    sum_recv,
    sum_recv_plane,
):
    rows_n, depth, width = sizes
    members = 2 * rows_n
    plane = members * width
    count = plane * depth
    rows, dims = ctx_ref.shape
    x = lax.axis_index("row")
    col = lax.axis_index("col")
    core = lax.rem(col, 2)
    y = lax.rem(lax.div(col, 2), width)
    z = lax.div(col, 2 * width)

    member = x * 2 + core
    own_plane = y * members + member
    me = y * depth + z

    def device(at_member, at_y, at_z):
        return (
            lax.div(at_member, 2),
            (at_z * width + at_y) * 2 + lax.rem(at_member, 2),
        )

    def z_peer(step):
        return device(member, y, lax.rem(z + step, depth))

    def y_peer(step):
        return device(member, lax.rem(y + step, width), z)

    def team_peer(step):
        return device(lax.rem(member + step, members), y, z)

    def plane_peer(step):
        place = lax.rem(own_plane + step, plane)
        return device(lax.rem(place, members), lax.div(place, members), z)

    any_peer = team_peer(1)

    barrier = pltpu.get_barrier_semaphore()

    def greet(peer):
        pl.semaphore_signal(barrier, inc=1, device_id=peer, device_id_type=MESH)

    loop(1, depth, lambda step: greet(z_peer(step)))
    loop(1, plane, lambda step: greet(plane_peer(step)))

    own = ctx_ref[...]
    blocks[me, 0:rows, :] = own
    team[member, 0:rows, :] = own
    own_wide = own.astype(F32)
    own_squares = jnp.sum(own_wide * own_wide, axis=1, keepdims=True) * (1.0 / dims)
    here = lax.broadcasted_iota(jnp.int32, (rows, rows), 0)
    there = lax.broadcasted_iota(jnp.int32, (rows, rows), 1)
    squares_row = jnp.sum(jnp.where(here == there, own_squares, 0.0), axis=0, keepdims=True)
    place = lax.broadcasted_iota(jnp.int32, (META // 2, rows), 0)
    picks = jnp.where((place >= 9) & (place <= 11), -0.5 * dims, 0.0).astype(BF16)
    picks = jnp.concatenate([picks] * members, axis=1)

    def pieces(value):
        high = jnp.floor(value * (1.0 / 512.0) + 0.5)
        return high, value - 512.0 * high

    policy_high, policy_low = pieces(policy_ref[...].astype(F32))
    logged_high, logged_low = pieces(logged_ref[...].astype(F32))
    square_1 = squares_row.astype(BF16).astype(F32)
    square_2 = (squares_row - square_1).astype(BF16).astype(F32)
    square_3 = squares_row - square_1 - square_2
    meta = jnp.concatenate(
        [
            policy_high,
            policy_low,
            jnp.broadcast_to(logged_high, (8, rows)),
            logged_low,
            square_1,
            square_2,
            square_3,
            jnp.zeros((4, rows), F32),
        ],
        axis=0,
    )
    blocks[me, rows : rows + META, :] = meta.astype(BF16)
    team[member, rows : rows + META, :] = meta.astype(BF16)
    total[...] = jnp.zeros_like(total)
    pl.semaphore_wait(barrier, (depth - 1) + (plane - 1))

    def remote(source, send_sem, recv_sem, peer):
        return pltpu.make_async_remote_copy(
            src_ref=source,
            dst_ref=source,
            send_sem=send_sem,
            recv_sem=recv_sem,
            device_id=peer,
            device_id_type=MESH,
        )

    def block_copy(index, peer):
        return remote(blocks.at[index], block_send, block_recv.at[index], peer)

    def to_y(index):
        loop(1, width, lambda step: block_copy(index, y_peer(step)).start())

    def team_copy(place, peer):
        return remote(team.at[place], team_send, team_recv.at[place], peer)

    wide = depth * rows

    def meta_of(group):
        base = group * depth
        return jnp.concatenate(
            [blocks[base + k, rows : rows + META, :].astype(F32) for k in range(depth)], axis=1
        )

    def first_pass(group):
        base = group * depth
        meta_all = meta_of(group)
        policy = (meta_all[0:8] * 512.0 + meta_all[8:16]).astype(jnp.int32)
        others = jnp.concatenate([blocks[base + k, 0:rows, :] for k in range(depth)], axis=0)
        squares = jnp.concatenate(
            [blocks[base + k, rows + META // 2 : rows + META, :] for k in range(depth)], axis=1
        )
        inner = dot(others, team_turned) + dot(squares, picks, 0)
        policy_feat = rounded(features(policy))
        gram = jnp.exp(inner * (2.0 / dims) - team_squares).astype(BF16)
        grams[group] = gram
        total[...] += dot(policy_feat, gram)

    loop(1, depth, lambda step: block_copy(me, z_peer(step)).start())
    to_y(me)
    loop(1, members, lambda step: team_copy(member, team_peer(step)).start())

    def from_z(step):
        index = y * depth + lax.rem(z + step, depth)
        block_copy(index, any_peer).wait_recv()
        to_y(index)

    loop(1, members, lambda k: team_copy(lax.rem(member + k, members), any_peer).wait_recv())
    turned_parts, square_parts, logged_parts = [], [], []
    for k in range(members):
        row_meta = team[k, rows : rows + META, :].astype(F32)
        turned_parts.append(team[k, 0:rows, :].astype(F32).T)
        square_parts.append(row_meta[25:26] + row_meta[26:27] + row_meta[27:28])
        logged_parts.append((row_meta[16:17] * 512.0 + row_meta[24:25]).astype(jnp.int32))
    team_turned = jnp.concatenate(turned_parts, axis=1).astype(BF16)
    team_squares = jnp.concatenate(square_parts, axis=1)
    team_logged = jnp.concatenate(logged_parts, axis=1)

    loop(1, depth, from_z)
    first_pass(y)

    def from_y(step):
        group = lax.rem(y + step, width)
        loop(0, depth, lambda k: block_copy(group * depth + k, any_peer).wait_recv())
        first_pass(group)

    loop(1, width, from_y)

    factor = NACT / (rows * count)
    own_feat = [
        part.astype(BF16).astype(F32)
        for part in features(jnp.broadcast_to(team_logged, (NPOL, members * rows)))
    ]

    def select():
        value = total[...]
        out = own_feat[0] * value[0:NPOL]
        for level in range(1, NACT):
            out += own_feat[level] * value[level * NPOL : (level + 1) * NPOL]
        return factor * out

    def show(group):
        meta_all = meta_of(group)
        shown = (meta_all[16:17] * 512.0 + meta_all[24:25]).astype(jnp.int32)
        logged_feat[group] = rounded(features(jnp.broadcast_to(shown, (NPOL, wide))))

    def part_copy(place, peer):
        return remote(parts.at[place], part_send, part_recv.at[place], peer)

    parts[member] = select()
    loop(1, members, lambda step: part_copy(member, team_peer(step)).start())
    loop(0, width, show)
    loop(1, members, lambda k: part_copy(lax.rem(member + k, members), any_peer).wait_recv())
    all_sides = jnp.sum(parts[...], axis=0)
    for k in range(members):
        team_sides[k] = all_sides[:, k * rows : (k + 1) * rows]
    right_side = team_sides[member]
    near[z] = right_side
    total[...] = jnp.zeros_like(total)

    def near_copy(place, peer):
        return remote(near.at[place], near_send, near_recv.at[place], peer)

    def side_copy(group, peer):
        return remote(sides.at[group], side_send, side_recv.at[group], peer)

    def second_pass(group):
        packed = sides[group].astype(F32)
        low = jnp.concatenate([packed[k * NPOL : (k + 1) * NPOL] for k in range(depth)], axis=1)
        feat = logged_feat[group].astype(F32)
        matched = (feat * jnp.concatenate([low] * NACT, axis=0)).astype(BF16)
        total[...] += dot(matched, grams[group])

    loop(1, depth, lambda step: near_copy(z, z_peer(step)).start())
    loop(1, depth, lambda step: near_copy(lax.rem(z + step, depth), any_peer).wait_recv())
    sides[y] = rounded([near[k] for k in range(depth)])
    loop(1, width, lambda step: side_copy(y, y_peer(step)).start())
    second_pass(y)

    def from_plane(step):
        group = lax.rem(y + step, width)
        side_copy(group, any_peer).wait_recv()
        second_pass(group)

    loop(1, width, from_plane)
    image_part = select()
    for k in range(members):
        image_out[k] = image_part[:, k * rows : (k + 1) * rows]
    image_in[member] = image_out[member]

    def image_copy(source, target, peer):
        return pltpu.make_async_remote_copy(
            src_ref=image_out.at[source],
            dst_ref=image_in.at[target],
            send_sem=image_send,
            recv_sem=image_recv.at[target],
            device_id=peer,
            device_id_type=MESH,
        )

    def send_image(step):
        image_copy(lax.rem(member + step, members), member, team_peer(step)).start()

    loop(1, members, send_image)
    own_square = right_side * right_side
    curved = image_out[0] * team_sides[0]
    for k in range(1, members):
        curved += image_out[k] * team_sides[k]

    lane = lax.broadcasted_iota(jnp.int32, (NPOL, rows), 1)
    sub = lax.broadcasted_iota(jnp.int32, (NPOL, rows), 0)

    def to_row(value, offset):
        column = jnp.sum(value, axis=1, keepdims=True)
        return jnp.sum(jnp.where(lane == sub + offset, column, 0.0), axis=0, keepdims=True)

    partial = (
        to_row(own_square, 0)
        + to_row(curved + RIDGE * own_square, NPOL)
        + to_row(reward_ref[...] * right_side, 2 * NPOL)
    )

    def all_sum(value, slots, recv, at, size, peer_of):
        slots[at] = value
        loop(
            1,
            size,
            lambda step: remote(slots.at[at], sum_send, recv.at[at], peer_of(step)).start(),
        )

        def arrive(step):
            place = lax.rem(at + step, size)
            remote(slots.at[place], sum_send, recv.at[place], any_peer).wait_recv()

        loop(1, size, arrive)
        return jnp.sum(slots[...], axis=0)

    partial = all_sum(partial, near_sums, sum_recv, z, depth, z_peer)
    partial = all_sum(partial, plane_sums, sum_recv_plane, own_plane, plane, plane_peer)

    def image_arrives(step):
        place = lax.rem(member + step, members)
        image_copy(place, place, any_peer).wait_recv()

    loop(1, members, image_arrives)
    image = jnp.sum(image_in[...], axis=0) + RIDGE * right_side

    def to_column(offset):
        spread_row = jnp.broadcast_to(partial, (NPOL, rows))
        return jnp.sum(jnp.where(lane == sub + offset, spread_row, 0.0), axis=1, keepdims=True)

    alpha = to_column(0) / to_column(NPOL)
    values_column = alpha * to_column(2 * NPOL) * (1.0 / (rows * count))
    values_row = jnp.sum(jnp.where(lane == sub, values_column, 0.0), axis=0, keepdims=True)
    results_ref[0:NPOL] = alpha * right_side
    results_ref[NPOL : 2 * NPOL] = right_side - alpha * image
    results_ref[2 * NPOL :] = jnp.broadcast_to(values_row, (NPOL, rows))

    blocks_sent = blocks.at[pl.ds(0, depth * width - 1)]
    remote(blocks_sent, block_send, block_recv.at[0], any_peer).wait_send()
    others = pl.ds(0, members - 1)
    remote(team.at[others], team_send, team_recv.at[0], any_peer).wait_send()
    remote(parts.at[others], part_send, part_recv.at[0], any_peer).wait_send()
    remote(image_out.at[others], image_send, image_recv.at[0], any_peer).wait_send()
    remote(near.at[pl.ds(0, depth - 1)], near_send, near_recv.at[0], any_peer).wait_send()
    remote(sides.at[pl.ds(0, width - 1)], side_send, side_recv.at[0], any_peer).wait_send()
    remote(
        near_sums.at[pl.ds(0, depth - 1)], sum_send, sum_recv.at[0], any_peer
    ).wait_send()
    remote(
        plane_sums.at[pl.ds(0, plane - 1)], sum_send, sum_recv_plane.at[0], any_peer
    ).wait_send()


def on_device(sizes, contexts, logged_actions, policy_actions, rewards):
    rows_n, depth, width = sizes
    rows, dims = contexts.shape
    members = 2 * rows_n
    plane = members * width
    vmem = pl.BlockSpec(memory_space=pltpu.VMEM)
    results = pl.pallas_call(
        functools.partial(kernel, sizes),
        out_shape=jax.ShapeDtypeStruct((3 * NPOL, rows), F32),
        in_specs=[vmem] * 4,
        out_specs=vmem,
        scratch_shapes=[
            pltpu.VMEM((width * depth, rows + META, dims), BF16),
            pltpu.VMEM((members, rows + META, dims), BF16),
            pltpu.VMEM((members, NPOL, members * rows), F32),
            pltpu.VMEM((members, NPOL, rows), F32),
            pltpu.VMEM((members, NPOL, rows), F32),
            pltpu.VMEM((members, NPOL, rows), F32),
            pltpu.VMEM((depth, NPOL, rows), F32),
            pltpu.VMEM((width, depth * NPOL, rows), BF16),
            pltpu.VMEM((width, depth * rows, members * rows), BF16),
            pltpu.VMEM((width, NPOL * NACT, depth * rows), BF16),
            pltpu.VMEM((NPOL * NACT, members * rows), F32),
            pltpu.VMEM((depth, 1, rows), F32),
            pltpu.VMEM((plane, 1, rows), F32),
            pltpu.SemaphoreType.DMA,
            pltpu.SemaphoreType.DMA((width * depth,)),
            pltpu.SemaphoreType.DMA,
            pltpu.SemaphoreType.DMA((members,)),
            pltpu.SemaphoreType.DMA,
            pltpu.SemaphoreType.DMA((members,)),
            pltpu.SemaphoreType.DMA,
            pltpu.SemaphoreType.DMA((members,)),
            pltpu.SemaphoreType.DMA,
            pltpu.SemaphoreType.DMA((depth,)),
            pltpu.SemaphoreType.DMA,
            pltpu.SemaphoreType.DMA((width,)),
            pltpu.SemaphoreType.DMA,
            pltpu.SemaphoreType.DMA((depth,)),
            pltpu.SemaphoreType.DMA((plane,)),
        ],
        compiler_params=pltpu.CompilerParams(
            collective_id=0, has_side_effects=True, vmem_limit_bytes=48 * 1024 * 1024
        ),
    )(contexts, logged_actions.reshape(1, rows), policy_actions.T, rewards.reshape(1, rows))
    return results[0:NPOL].T, results[NPOL : 2 * NPOL].T, results[2 * NPOL, 0:NPOL]


def solution(mesh):
    rows_n, cols = mesh.shape["row"], mesh.shape["col"]
    depth = 4 if (cols // 2) % 4 == 0 else 1
    sizes = (rows_n, depth, cols // 2 // depth)
    placed = (
        P(("row", "col"), None),
        P(("row", "col")),
        P(("row", "col"), None),
        P(("row", "col")),
    )
    return jax.shard_map(
        functools.partial(on_device, sizes),
        mesh=mesh,
        in_specs=placed,
        out_specs=(P(("row", "col"), None), P(("row", "col"), None), P()),
        check_vma=False,
    )
```

time: 36.7 us -> 34.5 us (0.940)
  Pallas kernels: 33.2 us -> 31 us
    pallas_call x1, Pallas kernels: 33.2 us -> 31 us  [on_device(): pl.pallas_call(functools.partial(kernel, sizes), out_shape=jax.ShapeDtype...]
where the time goes in v6:
time: 34.5 us; the launch traced here: 34.2 us
  Pallas kernels  31 us (90%)
  local copies, waits for them, and re-layouts  2.54 us (7%)
  between operations  0.67 us (2%)
    pallas_call x1, Pallas kernels, on_device(): pl.pallas_call(functools.partial(kernel, sizes), out_shape=jax.ShapeDtype...  31 us
    unnamed x8, local copies, waits for them, and re-layouts  1.43 us

profile of v6, /device:TPU:0, one launch (start us, length us, event | category | flops | bytes accessed | tf_op | source)
XLA Modules:
  0.0 34.2 jit_solution(2249403820362099675)
XLA Ops:
  0.6 0.0 copy-start.1
  0.6 0.0 copy-start.2
  0.7 0.0 copy-start.3
  0.7 0.7 %copy-done.1 = s32[128,8]{0,1:T(8,128)S(1)} copy-done((s32[128,8]{0,1:T(8,128)S(1)}, s32[128,8]{0,1:T(8,128)}, u32[]{:S(2)}) %copy-start.1) | copy-done | bytes 4120
  1.3 0.0 copy-done.2
  1.3 0.0 copy-done.3
  1.3 0.0 copy-start
  1.3 0.8 %copy-done = bf16[128,128]{1,0:T(8,128)(2,1)S(1)} copy-done((bf16[128,128]{1,0:T(8,128)(2,1)S(1)}, bf16[128,128]{1,0:T(8,128)(2,1)}, u32[]{:S(2)}) %copy-start) | copy-done | bytes 32792
  2.1 31.0 %shard_map.67 = f32[24,128]{1,0:T(8,128)S(1)} custom-call(bf16[128,128]{1,0:T(8,128)(2,1)S(1)} %copy-done, s32[1,128]{1,0:T(1,128)S(1)} %bitcast.10, s32[8,128]{1,0:T(8,128)S(1)} %bitcast.9, f32[1,128]{1,0:T(1,128)S(1)} %bitcast.11), custom_call_target="tpu_custom_call" | custom-call | tf_op jit(solution)/shard_map/pallas_call | solution.py:413
  33.1 0.6 %slice_bitcast_fusion = (f32[128,8]{0,1:T(8,128)}, f32[128,8]{0,1:T(8,128)}) fusion(f32[24,128]{1,0:T(8,128)S(1)} %shard_map.67), kind=kLoop, calls=%fused_computation | loop fusion | bytes 16384 | tf_op jit(solution)/shard_map/transpose | solution.py:452
  33.7 0.5 %slice_bitcast_fusion.2 = f32[8]{0:T(128)} fusion(f32[24,128]{1,0:T(8,128)S(1)} %shard_map.67), kind=kLoop, calls=%fused_computation.2 | loop fusion | bytes 64 | tf_op jit(solution)/shard_map/squeeze | solution.py:452
Async XLA Ops:
  0.6 0.7 %copy-start.1 = (s32[128,8]{0,1:T(8,128)S(1)}, s32[128,8]{0,1:T(8,128)}, u32[]{:S(2)}) copy-start(s32[128,8]{0,1:T(8,128)} %param.6) | copy-start | bytes 12292
  0.6 0.7 %copy-start.2 = (s32[128]{0:T(128)S(1)}, s32[128]{0:T(128)}, u32[]{:S(2)}) copy-start(s32[128]{0:T(128)} %param.5) | copy-start | bytes 1540
  0.7 0.7 %copy-start.3 = (f32[128]{0:T(128)S(1)}, f32[128]{0:T(128)}, u32[]{:S(2)}) copy-start(f32[128]{0:T(128)} %param.7) | copy-start | bytes 1540
  1.3 0.8 %copy-start = (bf16[128,128]{1,0:T(8,128)(2,1)S(1)}, bf16[128,128]{1,0:T(8,128)(2,1)}, u32[]{:S(2)}) copy-start(bf16[128,128]{1,0:T(8,128)(2,1)} %ctx_ref.1) | copy-start | bytes 98308

commit v7 on v6

--- a/solution.py
+++ b/solution.py
@@ -104,26 +104,27 @@
     sum_recv,
     sum_recv_plane,
 ):
-    rows_n, depth, width = sizes
-    members = 2 * rows_n
+    rows_n, depth, full, fold = sizes
+    width = full // fold
+    members = 2 * rows_n * fold
     plane = members * width
     count = plane * depth
     rows, dims = ctx_ref.shape
     x = lax.axis_index("row")
     col = lax.axis_index("col")
     core = lax.rem(col, 2)
-    y = lax.rem(lax.div(col, 2), width)
-    z = lax.div(col, 2 * width)
-
-    member = x * 2 + core
+    at_full = lax.rem(lax.div(col, 2), full)
+    y = lax.div(at_full, fold)
+    z = lax.div(col, 2 * full)
+
+    member = (x * fold + lax.rem(at_full, fold)) * 2 + core
     own_plane = y * members + member
     me = y * depth + z
 
     def device(at_member, at_y, at_z):
-        return (
-            lax.div(at_member, 2),
-            (at_z * width + at_y) * 2 + lax.rem(at_member, 2),
-        )
+        place = lax.div(at_member, 2)
+        line = at_y * fold + lax.rem(place, fold)
+        return (lax.div(place, fold), (at_z * full + line) * 2 + lax.rem(at_member, 2))
 
     def z_peer(step):
         return device(member, y, lax.rem(z + step, depth))
@@ -395,7 +396,9 @@
     remote(parts.at[others], part_send, part_recv.at[0], any_peer).wait_send()
     remote(image_out.at[others], image_send, image_recv.at[0], any_peer).wait_send()
     remote(near.at[pl.ds(0, depth - 1)], near_send, near_recv.at[0], any_peer).wait_send()
-    remote(sides.at[pl.ds(0, width - 1)], side_send, side_recv.at[0], any_peer).wait_send()
+    if width > 1:
+        sides_sent = sides.at[pl.ds(0, width - 1)]
+        remote(sides_sent, side_send, side_recv.at[0], any_peer).wait_send()
     remote(
         near_sums.at[pl.ds(0, depth - 1)], sum_send, sum_recv.at[0], any_peer
     ).wait_send()
@@ -405,9 +408,10 @@
 
 
 def on_device(sizes, contexts, logged_actions, policy_actions, rewards):
-    rows_n, depth, width = sizes
+    rows_n, depth, full, fold = sizes
+    width = full // fold
     rows, dims = contexts.shape
-    members = 2 * rows_n
+    members = 2 * rows_n * fold
     plane = members * width
     vmem = pl.BlockSpec(memory_space=pltpu.VMEM)
     results = pl.pallas_call(
@@ -455,7 +459,9 @@
 def solution(mesh):
     rows_n, cols = mesh.shape["row"], mesh.shape["col"]
     depth = 4 if (cols // 2) % 4 == 0 else 1
-    sizes = (rows_n, depth, cols // 2 // depth)
+    width = cols // 2 // depth
+    fold = width if rows_n * width <= 4 else 1
+    sizes = (rows_n, depth, width, fold)
     placed = (
         P(("row", "col"), None),
         P(("row", "col")),

time: 34.5 us -> 31 us (0.90)
  Pallas kernels: 31 us -> 27.6 us
    pallas_call x1, Pallas kernels: 31 us -> 27.6 us  [on_device(): pl.pallas_call(functools.partial(kernel, sizes), out_shape=jax.ShapeDtype...]
where the time goes in v7:
time: 31 us; the launch traced here: 30.8 us
  Pallas kernels  27.6 us (89%)
  local copies, waits for them, and re-layouts  2.54 us (8%)
  between operations  0.67 us (2%)
    pallas_call x1, Pallas kernels, on_device(): pl.pallas_call(functools.partial(kernel, sizes), out_shape=jax.ShapeDtype...  27.6 us
    unnamed x8, local copies, waits for them, and re-layouts  1.43 us

profile of v7, /device:TPU:0, one launch (start us, length us, event | category | flops | bytes accessed | tf_op | source)
XLA Modules:
  0.0 30.8 jit_solution(14464520362791483278)
XLA Ops:
  0.6 0.0 copy-start.1
  0.6 0.0 copy-start.2
  0.7 0.0 copy-start.3
  0.7 0.7 %copy-done.1 = s32[128,8]{0,1:T(8,128)S(1)} copy-done((s32[128,8]{0,1:T(8,128)S(1)}, s32[128,8]{0,1:T(8,128)}, u32[]{:S(2)}) %copy-start.1) | copy-done | bytes 4120
  1.3 0.0 copy-done.2
  1.3 0.0 copy-done.3
  1.3 0.0 copy-start
  1.3 0.8 %copy-done = bf16[128,128]{1,0:T(8,128)(2,1)S(1)} copy-done((bf16[128,128]{1,0:T(8,128)(2,1)S(1)}, bf16[128,128]{1,0:T(8,128)(2,1)}, u32[]{:S(2)}) %copy-start) | copy-done | bytes 32792
  2.1 27.6 %shard_map.67 = f32[24,128]{1,0:T(8,128)S(1)} custom-call(bf16[128,128]{1,0:T(8,128)(2,1)S(1)} %copy-done, s32[1,128]{1,0:T(1,128)S(1)} %bitcast.10, s32[8,128]{1,0:T(8,128)S(1)} %bitcast.9, f32[1,128]{1,0:T(1,128)S(1)} %bitcast.11), custom_call_target="tpu_custom_call" | custom-call | tf_op jit(solution)/shard_map/pallas_call | solution.py:417
  29.7 0.6 %slice_bitcast_fusion = (f32[128,8]{0,1:T(8,128)}, f32[128,8]{0,1:T(8,128)}) fusion(f32[24,128]{1,0:T(8,128)S(1)} %shard_map.67), kind=kLoop, calls=%fused_computation | loop fusion | bytes 16384 | tf_op jit(solution)/shard_map/transpose | solution.py:456
  30.3 0.5 %slice_bitcast_fusion.2 = f32[8]{0:T(128)} fusion(f32[24,128]{1,0:T(8,128)S(1)} %shard_map.67), kind=kLoop, calls=%fused_computation.2 | loop fusion | bytes 64 | tf_op jit(solution)/shard_map/squeeze | solution.py:456
Async XLA Ops:
  0.6 0.7 %copy-start.1 = (s32[128,8]{0,1:T(8,128)S(1)}, s32[128,8]{0,1:T(8,128)}, u32[]{:S(2)}) copy-start(s32[128,8]{0,1:T(8,128)} %param.6) | copy-start | bytes 12292
  0.6 0.7 %copy-start.2 = (s32[128]{0:T(128)S(1)}, s32[128]{0:T(128)}, u32[]{:S(2)}) copy-start(s32[128]{0:T(128)} %param.5) | copy-start | bytes 1540
  0.7 0.7 %copy-start.3 = (f32[128]{0:T(128)S(1)}, f32[128]{0:T(128)}, u32[]{:S(2)}) copy-start(f32[128]{0:T(128)} %param.7) | copy-start | bytes 1540
  1.3 0.8 %copy-start = (bf16[128,128]{1,0:T(8,128)(2,1)S(1)}, bf16[128,128]{1,0:T(8,128)(2,1)}, u32[]{:S(2)}) copy-start(bf16[128,128]{1,0:T(8,128)(2,1)} %ctx_ref.1) | copy-start | bytes 98308
